TPU v7x, 256 devices: a whole 4x4x8 slice. The times are simulated.
256 devices in a mesh: section: 32 (over z, y), dp: 8 (over x, core).
Axes of the slice: x: 4, y: 4, z: 8, core: 2. Of those that a mesh axis runs over, the one named last changes fastest.
Arguments:
- loaded: bfloat16 [1024, 2560], P(('section', 'dp')), may hold values from -6 to 6
- positions: int32 [1024], P(('section', 'dp')), may hold values from 0 to 127, as said below
- span_lengths: int32 [8, 6], P('dp'), may hold values from 1 to 32, 128 in all within a row
- visit_embed: bfloat16 [6, 2560], replicated, may hold values from -6 to 6
- w_query: bfloat16 [81920, 1280], P(('section', 'dp')), may hold values from -0.125 to 0.125
- w_key: bfloat16 [81920, 1280], P(('section', 'dp')), may hold values from -0.125 to 0.125
- w_value: bfloat16 [81920, 1280], P(('section', 'dp')), may hold values from -0.125 to 0.125
- w_out: bfloat16 [40960, 2560], P(('section', 'dp')), may hold values from -0.5 to 0.5
- norm_gain: float32 [81920], P('section'), may hold values from 0.25 to 1.75
Outputs:
- section_out: bfloat16 [32, 1024, 2560], P('section', 'dp')
Inputs may be any that keep to these rules, and one draw needn't show every extreme that they name: For each history, its 128 positions appear once each among the loaded rows of its devices.
All inputs are finite; a program needn't handle non-finite values.
Results may differ from a plain program's by a relative error of at most 0.03.
Values may be sent and summed in bfloat16 or wider, within the bound.
No kernel may reach another device: no remote copies, remote signals or barrier semaphores. Data moves between devices by JAX's collectives and lax.ppermute only.
A program may use at most 128 MiB of HBM per device.

v0:
```python
import jax
import jax.numpy as jnp
from jax import lax
from jax.sharding import PartitionSpec as P

AHEADS = 16
LMAX = 32


def from_behind(value, axis, steps):
    count = lax.axis_size(axis)
    first, last = (max(0, -steps), min(count, count - steps))
    return lax.ppermute(value, axis, [(source, source + steps) for source in range(first, last)])


def shards(loaded, positions, span_lengths, visit_embed, w_query, w_key, w_value, w_out, norm_gain):
    width = loaded.shape[1]
    seq = loaded.shape[0] * lax.axis_size("section")
    index_col = jnp.arange(seq, dtype=jnp.int32)
    gathered, owners = (
        lax.all_gather(loaded, "section", axis=0, tiled=True),
        lax.all_gather(positions, "section", axis=0, tiled=True),
    )
    placing = (index_col[:, None] == owners[None, :]).astype(jnp.bfloat16)
    ordered = jnp.dot(placing, gathered, preferred_element_type=jnp.float32)
    lengths = span_lengths[0]
    nchunk = lengths.shape[0]
    ends = jnp.cumsum(lengths)
    starts = ends - lengths
    visit_id = jnp.sum((index_col[:, None] >= ends[None, :]).astype(jnp.int32), axis=1)
    visit_hot = (visit_id[:, None] == jnp.arange(nchunk, dtype=jnp.int32)[None, :]).astype(
        jnp.bfloat16
    )
    visit_rows = jnp.dot(visit_hot, visit_embed, preferred_element_type=jnp.float32)
    start_x = (ordered + visit_rows).astype(jnp.bfloat16)
    padded_in = jnp.concatenate([start_x, jnp.zeros((LMAX, width), jnp.bfloat16)], axis=0)
    query_full, key_full, value_full, out_full = (
        lax.all_gather(w_query, "dp", axis=0, tiled=True),
        lax.all_gather(w_key, "dp", axis=0, tiled=True),
        lax.all_gather(w_value, "dp", axis=0, tiled=True),
        lax.all_gather(w_out, "dp", axis=0, tiled=True),
    )
    att_width = query_full.shape[1]
    head_count = AHEADS
    head_size = att_width // head_count
    cache_rows = seq + LMAX
    cache_index = jnp.arange(cache_rows, dtype=jnp.int32)
    rank_here = lax.axis_index("section")
    depth_count = lax.axis_size("section")
    local_rows = jnp.arange(LMAX, dtype=jnp.int32)

    def run_layer(operands):
        x_block, length, start, key_cache, value_cache = operands
        floats = x_block.astype(jnp.float32)
        normed = (
            floats / jnp.sqrt(jnp.mean(floats * floats, axis=1, keepdims=True) + 1e-05) * norm_gain
        ).astype(jnp.bfloat16)
        query = jnp.dot(normed, query_full, preferred_element_type=jnp.float32).astype(jnp.bfloat16)
        keys_new = jnp.dot(normed, key_full, preferred_element_type=jnp.float32).astype(
            jnp.bfloat16
        )
        values_new = jnp.dot(normed, value_full, preferred_element_type=jnp.float32).astype(
            jnp.bfloat16
        )
        key_cache = lax.dynamic_update_slice_in_dim(key_cache, keys_new, start, 0)
        value_cache = lax.dynamic_update_slice_in_dim(value_cache, values_new, start, 0)
        query_heads = query.reshape(LMAX, head_count, head_size)
        key_heads = key_cache.reshape(cache_rows, head_count, head_size)
        value_heads = value_cache.reshape(cache_rows, head_count, head_size)
        scores = jnp.einsum(
            "ihd,jhd->hij", query_heads, key_heads, preferred_element_type=jnp.float32
        ) / jnp.sqrt(jnp.float32(head_size))
        allowed = cache_index[None, :] <= (start + local_rows)[:, None]
        scores = jnp.where(allowed[None], scores, -1e30)
        probs = jax.nn.softmax(scores, axis=-1).astype(jnp.bfloat16)
        attended = (
            jnp.einsum("hij,jhd->ihd", probs, value_heads, preferred_element_type=jnp.float32)
            .reshape(LMAX, att_width)
            .astype(jnp.bfloat16)
        )
        mixed = jnp.dot(attended, out_full, preferred_element_type=jnp.float32)
        result = (floats + mixed).astype(jnp.bfloat16)
        result = jnp.where((local_rows < length)[:, None], result, jnp.zeros_like(result))
        return (result, key_cache, value_cache)

    def spare_layer(operands):
        x_block, length, start, key_cache, value_cache = operands
        return (jnp.zeros((LMAX, width), jnp.bfloat16), key_cache, value_cache)

    def turn(step, carry):
        received, out_buffer, key_cache, value_cache = carry
        block = step - rank_here
        active = (block >= 0) & (block < nchunk)
        safe = jnp.clip(block, 0, nchunk - 1)
        start = starts[safe]
        length = lengths[safe]
        first_in = lax.dynamic_slice_in_dim(padded_in, start, LMAX, 0)
        x_block = jnp.where(rank_here == 0, first_in, received)
        result, key_cache, value_cache = lax.cond(
            active, run_layer, spare_layer, (x_block, length, start, key_cache, value_cache)
        )
        current = lax.dynamic_slice_in_dim(out_buffer, start, LMAX, 0)
        keep = jnp.where(active & (local_rows < length)[:, None], result, current)
        out_buffer = lax.dynamic_update_slice_in_dim(out_buffer, keep, start, 0)
        sent = from_behind(result, "section", 1)
        return (sent, out_buffer, key_cache, value_cache)

    init = (
        jnp.zeros((LMAX, width), jnp.bfloat16),
        jnp.zeros((cache_rows, width), jnp.bfloat16),
        jnp.zeros((cache_rows, att_width), jnp.bfloat16),
        jnp.zeros((cache_rows, att_width), jnp.bfloat16),
    )
    final = lax.fori_loop(0, nchunk + depth_count - 1, turn, init)
    return final[1][:seq][None]


def solution(mesh):
    placed = (
        P(("section", "dp"), None),
        P(("section", "dp")),
        P("dp", None),
        P(),
        P(("section", "dp"), None),
        P(("section", "dp"), None),
        P(("section", "dp"), None),
        P(("section", "dp"), None),
        P("section"),
    )
    return jax.shard_map(
        shards, mesh=mesh, in_specs=placed, out_specs=P("section", "dp", None), check_vma=False
    )
```

profile of v0, /device:TPU:248, one launch (start us, length us, event | category | flops | bytes accessed | tf_op | source)
XLA Modules:
  0.0 1391.1 jit_solution(18089515454409950184)
XLA Ops:
  10.2 47.3 %all-gather = bf16[32,4,2560]{2,1,0:T(4,128)(2,1)S(1)} all-gather(bf16[1,4,2560]{2,1,0:T(4,128)(2,1)} %bitcast.26), channel_id=1, replica_groups=mesh['section'=32,'dp'=8] {'section'}, dimensions={0}, use_global_device_ids=true | all-gather | bytes 675840 | tf_op jit(solution)/shard_map/all_gather | solution.py:21
  60.5 18.2 %all-reduce.1 = s32[128]{0:T(128)S(1)} all-reduce(s32[128]{0:T(128)S(1)} %dynamic-update-slice), channel_id=1, replica_groups=mesh['section'=32,'dp'=8] {'section'}, use_global_device_ids=true, to_apply=%add.1 | all-reduce | flops 128 | bytes 1024
  80.4 20.0 %all-gather.10.cloned.1.call-done = bf16[2560,1280]{1,0:T(8,128)(2,1)} async-done(((bf16[320,1280]{1,0:T(8,128)(2,1)}), bf16[2560,1280]{1,0:T(8,128)(2,1)}) %all-gather.10.cloned.1.call-update) | async-done | bytes 6553616 | tf_op jit(solution)/shard_map/all_gather | solution.py:39
  100.4 46.5 %all-gather.6.cloned.1.call-done = bf16[2560,1280]{1,0:T(8,128)(2,1)} async-done(((bf16[320,1280]{1,0:T(8,128)(2,1)}), bf16[2560,1280]{1,0:T(8,128)(2,1)}) %all-gather.6.cloned.1.call-update) | async-done | bytes 6553616 | tf_op jit(solution)/shard_map/all_gather | solution.py:40
  147.0 46.4 %all-gather.12.cloned.1.call-done = bf16[1280,2560]{1,0:T(8,128)(2,1)} async-done(((bf16[160,2560]{1,0:T(8,128)(2,1)}), bf16[1280,2560]{1,0:T(8,128)(2,1)}) %all-gather.12.cloned.1.call-update) | async-done | bytes 6553616 | tf_op jit(solution)/shard_map/all_gather | solution.py:41
  193.5 1190.1 %while.22 = (s32[]{:T(128)}, bf16[32,2560]{1,0:T(8,128)(2,1)S(1)}, bf16[160,2560]{1,0:T(8,128)(2,1)S(1)}, bf16[160,1280]{1,0:T(8,128)(2,1)S(1)}, bf16[160,1280]{...) while((s32[]{:T(128)}, bf16[32,2560]{1,0:T(8,128)(2,1)S(1)}, ...), condition=%wide.region_8.9_spmd.clone.clone, body=%wide.region_2.8_spmd.clone.clone.sunk | while | flops 867538880 | bytes 86228328 | solution.py:114
  318.5 6.9 collective-permute-done
  332.2 7.9 collective-permute-done
  347.0 7.0 collective-permute-done
  449.1 6.1 collective-permute-done
  462.1 7.7 collective-permute-done
  476.6 7.7 collective-permute-done
  579.3 592.1 %collective-permute-done = bf16[32,2560]{1,0:T(8,128)(2,1)S(1)} collective-permute-done((bf16[32,2560]{1,0:T(8,128)(2,1)S(1)}, bf16[32,2560]{1,0:T(8,128)(2,1)S(1)}, u32[]{:S(2)}, u32[]{:S(2)}) %collective-permute-start) | collective-permute-done | bytes 163872 | tf_op jit(solution)/shard_map/while/body/eval_jaxpr/ppermute | solution.py:13
  1174.7 21.7 %conditional.4 = (bf16[32,2560]{1,0:T(8,128)(2,1)S(1)}, bf16[160,1280]{1,0:T(8,128)(2,1)S(1)}, bf16[160,1280]{1,0:T(8,128)(2,1)S(1)}) conditional(s32[]{:T(128)} %convert_element_type.88, (bf16[160,1280]{1,0:T(8,128)(2,1)S(1)}, bf16[160,1280]{1,0:T(8,128)(2,1)S(1)}) %tuple.55, (s32[]{:T(128)}, s32[32]{0:T(128)S(1)}, pred[]{:T(512)}, ...), branch_computations={%region_3.3_spmd, %region_4.7_spmd} | conditional | flops 867456896 | bytes 84752440 | solution.py:99
  1199.9 7.1 collective-permute-done
  1210.4 21.7 %conditional.4 = (bf16[32,2560]{1,0:T(8,128)(2,1)S(1)}, bf16[160,1280]{1,0:T(8,128)(2,1)S(1)}, bf16[160,1280]{1,0:T(8,128)(2,1)S(1)}) conditional(s32[]{:T(128)} %convert_element_type.88, (bf16[160,1280]{1,0:T(8,128)(2,1)S(1)}, bf16[160,1280]{1,0:T(8,128)(2,1)S(1)}) %tuple.55, (s32[]{:T(128)}, s32[32]{0:T(128)S(1)}, pred[]{:T(512)}, ...), branch_computations={%region_3.3_spmd, %region_4.7_spmd} | conditional | flops 867456896 | bytes 84752440 | solution.py:99
  1235.5 7.1 collective-permute-done
  1246.0 21.7 %conditional.4 = (bf16[32,2560]{1,0:T(8,128)(2,1)S(1)}, bf16[160,1280]{1,0:T(8,128)(2,1)S(1)}, bf16[160,1280]{1,0:T(8,128)(2,1)S(1)}) conditional(s32[]{:T(128)} %convert_element_type.88, (bf16[160,1280]{1,0:T(8,128)(2,1)S(1)}, bf16[160,1280]{1,0:T(8,128)(2,1)S(1)}) %tuple.55, (s32[]{:T(128)}, s32[32]{0:T(128)S(1)}, pred[]{:T(512)}, ...), branch_computations={%region_3.3_spmd, %region_4.7_spmd} | conditional | flops 867456896 | bytes 84752440 | solution.py:99
  1271.2 7.1 collective-permute-done
  1281.6 21.7 %conditional.4 = (bf16[32,2560]{1,0:T(8,128)(2,1)S(1)}, bf16[160,1280]{1,0:T(8,128)(2,1)S(1)}, bf16[160,1280]{1,0:T(8,128)(2,1)S(1)}) conditional(s32[]{:T(128)} %convert_element_type.88, (bf16[160,1280]{1,0:T(8,128)(2,1)S(1)}, bf16[160,1280]{1,0:T(8,128)(2,1)S(1)}) %tuple.55, (s32[]{:T(128)}, s32[32]{0:T(128)S(1)}, pred[]{:T(512)}, ...), branch_computations={%region_3.3_spmd, %region_4.7_spmd} | conditional | flops 867456896 | bytes 84752440 | solution.py:99
  1306.8 7.1 collective-permute-done
  1317.3 21.7 %conditional.4 = (bf16[32,2560]{1,0:T(8,128)(2,1)S(1)}, bf16[160,1280]{1,0:T(8,128)(2,1)S(1)}, bf16[160,1280]{1,0:T(8,128)(2,1)S(1)}) conditional(s32[]{:T(128)} %convert_element_type.88, (bf16[160,1280]{1,0:T(8,128)(2,1)S(1)}, bf16[160,1280]{1,0:T(8,128)(2,1)S(1)}) %tuple.55, (s32[]{:T(128)}, s32[32]{0:T(128)S(1)}, pred[]{:T(512)}, ...), branch_computations={%region_3.3_spmd, %region_4.7_spmd} | conditional | flops 867456896 | bytes 84752440 | solution.py:99
  1342.4 8.9 collective-permute-done
  1354.7 21.7 %conditional.4 = (bf16[32,2560]{1,0:T(8,128)(2,1)S(1)}, bf16[160,1280]{1,0:T(8,128)(2,1)S(1)}, bf16[160,1280]{1,0:T(8,128)(2,1)S(1)}) conditional(s32[]{:T(128)} %convert_element_type.88, (bf16[160,1280]{1,0:T(8,128)(2,1)S(1)}, bf16[160,1280]{1,0:T(8,128)(2,1)S(1)}) %tuple.55, (s32[]{:T(128)}, s32[32]{0:T(128)S(1)}, pred[]{:T(512)}, ...), branch_computations={%region_3.3_spmd, %region_4.7_spmd} | conditional | flops 867456896 | bytes 84752440 | solution.py:99
  (551 shorter events, 434.0 us)
Async XLA Ops:
  6.5 73.9 %all-gather.8.cloned.1.call-start = ((), (), s32[]{:S(2)}) async-start(), calls=%async_computation.1 | async-start | bytes 7372800 | tf_op jit(solution)/shard_map/all_gather | solution.py:38
  7.3 93.2 %all-gather.10.cloned.1.call-start = ((), (), s32[]{:S(2)}) async-start(), calls=%async_computation.2 | async-start | bytes 7372800 | tf_op jit(solution)/shard_map/all_gather | solution.py:39
  8.0 139.0 %all-gather.6.cloned.1.call-start = ((), (), s32[]{:S(2)}) async-start(), calls=%async_computation | async-start | bytes 7372800 | tf_op jit(solution)/shard_map/all_gather | solution.py:40
  8.7 184.6 %all-gather.12.cloned.1.call-start = ((), (), s32[]{:S(2)}) async-start(), calls=%async_computation.3 | async-start | bytes 7372800 | tf_op jit(solution)/shard_map/all_gather | solution.py:41
  251.5 9.3 collective-permute-start
  264.2 9.3 collective-permute-start
  276.9 9.3 collective-permute-start
  289.7 9.3 collective-permute-start
  315.1 10.3 collective-permute-start
  328.8 11.3 collective-permute-start
  343.6 10.4 collective-permute-start
  357.4 9.5 collective-permute-start
  433.0 9.3 collective-permute-start
  445.7 9.5 collective-permute-start
  458.7 11.1 collective-permute-start
  473.2 11.1 collective-permute-start
  487.7 9.4 collective-permute-start
  563.2 9.3 collective-permute-start
  575.9 595.5 %collective-permute-start = (bf16[32,2560]{1,0:T(8,128)(2,1)S(1)}, bf16[32,2560]{1,0:T(8,128)(2,1)S(1)}, u32[]{:S(2)}, u32[]{:S(2)}) collective-permute-start(bf16[32,2560]{1,0:T(8,128)(2,1)S(1)} %get-tuple-element.640), channel_id=1, source_target_pairs={{0,8},{8,16},{16,24},{24,32},{32,40},{40,48},{48,56},{56,64},{64,7... | collective-permute-start | bytes 491528 | tf_op jit(solution)/shard_map/while/body/eval_jaxpr/ppermute | solution.py:13
  1196.5 10.5 collective-permute-start
  1232.1 10.5 collective-permute-start
  1267.8 10.5 collective-permute-start
  1303.4 10.5 collective-permute-start
  1339.0 12.3 collective-permute-start
  (32 other events, 556.0 us)
Sparse Core Ops, SparseCore 0:
  9.2 44.6 all-gather.7
  55.7 44.6 all-gather.9
  102.3 44.6 all-gather.5
  148.7 44.6 all-gather.11
where the time goes:
time: 1390 us
  waiting for transfers between devices  924 us (66%)
  local copies, waits for them, and re-layouts  127 us (9%)
  loops' own time  93.3 us (7%)
  matrix products  75 us (5%)
  blocking collectives  65.5 us (5%)
  starting transfers between devices  47.9 us (3%)
  other arithmetic  45.3 us (3%)
    ppermute x37, waiting for transfers between devices, from_behind(): lax.ppermute(value, axis, [(source, source + steps) for source in range(f...  808 us
    another operation x1, loops' own time, shards(): final = lax.fori_loop(0, nchunk + depth_count - 1, turn, init)  79.1 us
    dynamic_update_slice x37, local copies, waits for them, and re-layouts, turn(): out_buffer = lax.dynamic_update_slice_in_dim(out_buffer, keep, start, 0)  51.9 us
    ppermute x37, starting transfers between devices, from_behind(): lax.ppermute(value, axis, [(source, source + steps) for source in range(f...  47.8 us
    all_gather x1, blocking collectives, shards(): lax.all_gather(loaded, 'section', axis=0, tiled=True)  47.3 us
    all_gather x1, waiting for transfers between devices, shards(): lax.all_gather(w_value, 'dp', axis=0, tiled=True)  46.5 us
    all_gather x1, waiting for transfers between devices, shards(): lax.all_gather(w_out, 'dp', axis=0, tiled=True)  46.4 us
  transfers between devices with their start and end apart: 41, of which 40 were waited for; matrix products, arithmetic and copies ran while one was open for 6% of the time, Pallas kernels for 0%

commit v1 on v0

v1 whole, which is shorter than its diff:
```python
import jax
import jax.numpy as jnp
from jax import lax
from jax.experimental import pallas as pl
from jax.experimental.pallas import tpu as pltpu
from jax.sharding import PartitionSpec as P

HEADS = 16
GROUP = 8
ROWS = 16
SKEW = 2
BF16 = jnp.bfloat16
F32 = jnp.float32


def in_vmem(value):
    return pltpu.with_memory_space_constraint(value, pltpu.VMEM)


def in_hbm(value):
    return pltpu.with_memory_space_constraint(value, pltpu.HBM)


VMEM_SPEC = pl.BlockSpec(memory_space=pltpu.VMEM)
SMEM_SPEC = pl.BlockSpec(memory_space=pltpu.SMEM)
HBM_SPEC = pl.BlockSpec(memory_space=pltpu.HBM)


def lane_shift(chips, steps):
    return [
        (x * 2 + c, ((x + steps) % chips) * 2 + c) for x in range(chips) for c in range(2)
    ]


def load_weights(chip, core, pieces):
    offsets = [(0, 0), (0, 1), (-1, 0), (-1, 1), (1, 0), (1, 1), (2, 0), (2, 1)]
    count = len(offsets)
    part = pieces[0][0].shape[0]
    att = pieces[0][0].shape[1]
    out_part, width = pieces[3][0].shape

    def body(where, *refs):
        sources = refs[: 4 * count]
        qkv, out, sems = refs[4 * count :]
        copies = []
        for k in range(4):
            for j, (away, other) in enumerate(offsets):
                x = lax.rem(where[0] + away + 4, 4)
                c = where[1] if other == 0 else 1 - where[1]
                spot = x * 2 + c
                if k < 3:
                    target = qkv.at[pl.ds(pl.multiple_of(spot * part, part), part), pl.ds(k * att, att)]
                else:
                    target = out.at[pl.ds(pl.multiple_of(spot * out_part, out_part), out_part), :]
                copies.append(pltpu.make_async_copy(sources[k * count + j], target, sems.at[k * count + j]))
        for copy in copies:
            copy.start()
        for copy in copies:
            copy.wait()

    flat = [in_hbm(piece) for group in pieces for piece in group]
    return pl.pallas_call(
        body,
        out_shape=(
            pltpu.VMEM((part * count, 3 * att), BF16),
            pltpu.VMEM((out_part * count, width), BF16),
        ),
        in_specs=[SMEM_SPEC] + [HBM_SPEC] * len(flat),
        out_specs=[VMEM_SPEC] * 2,
        scratch_shapes=[pltpu.SemaphoreType.DMA((4 * count,))],
        compiler_params=pltpu.CompilerParams(vmem_limit_bytes=2 * 2**20),
        name="load_weights",
    )(jnp.stack([chip, core]), *flat)


def step_body(step, blocks, where, x_in, start_x, gain, qkv, out, k_in, v_in, o_in, y, keys, values, outs):
    section = where[2]
    block = step - SKEW * section
    att, width = out.shape
    seq = keys.shape[0]
    size = att // HEADS
    wide = GROUP * size

    @pl.when((block >= 0) & (block < blocks))
    def _():
        row = pl.multiple_of(block * ROWS, ROWS)
        rows = pl.ds(row, ROWS)
        first = (jnp.zeros((ROWS, width), jnp.int32) + section) == 0
        x = jnp.where(first, start_x[rows, :].astype(F32), x_in[...].astype(F32))
        normed = (
            x / jnp.sqrt(jnp.mean(x * x, axis=1, keepdims=True) + 1e-05) * gain[...]
        ).astype(BF16)
        mixed = jnp.dot(normed, qkv[...], preferred_element_type=F32).astype(BF16)
        query = mixed[:, :att]
        keys[rows, :] = mixed[:, att : 2 * att]
        values[rows, :] = mixed[:, 2 * att :]
        lane = lax.broadcasted_iota(jnp.int32, (GROUP, ROWS, wide), 2)
        head = lax.broadcasted_iota(jnp.int32, (GROUP, ROWS, wide), 0)
        own = (lane >= head * size) & (lane < (head + 1) * size)
        key_at = lax.broadcasted_iota(jnp.int32, (GROUP, ROWS, seq), 2)
        query_at = lax.broadcasted_iota(jnp.int32, (GROUP, ROWS, seq), 1) + row
        allowed = (key_at <= query_at).reshape(GROUP * ROWS, seq)
        joined = []
        for g in range(HEADS // GROUP):
            cols = slice(g * wide, (g + 1) * wide)
            spread = jnp.where(
                own, jnp.broadcast_to(query[:, cols][None], (GROUP, ROWS, wide)), jnp.zeros((), BF16)
            ).reshape(GROUP * ROWS, wide)
            scores = lax.dot_general(
                spread, keys[:, cols], (((1,), (1,)), ((), ())), preferred_element_type=F32
            )
            scores = jnp.where(allowed, scores / jnp.sqrt(F32(size)), -1e30)
            powers = jnp.exp(scores - jnp.max(scores, axis=1, keepdims=True))
            probs = (powers / jnp.sum(powers, axis=1, keepdims=True)).astype(BF16)
            mixed_v = jnp.dot(probs, values[:, cols], preferred_element_type=F32)
            mixed_v = jnp.where(own, mixed_v.reshape(GROUP, ROWS, wide), 0.0)
            joined.append(jnp.sum(mixed_v, axis=0).astype(BF16))
        attended = jnp.concatenate(joined, axis=1)
        result = (x + jnp.dot(attended, out[...], preferred_element_type=F32)).astype(BF16)
        y[...] = result
        outs[rows, :] = result


def run_step(step, blocks, where, x_in, start_x, gain, qkv, out, keys, values, outs):
    width = out.shape[1]

    def body(*refs):
        step_body(step, blocks, *refs)

    return pl.pallas_call(
        body,
        out_shape=(
            pltpu.VMEM((ROWS, width), BF16),
            pltpu.VMEM(keys.shape, BF16),
            pltpu.VMEM(values.shape, BF16),
            pltpu.VMEM(outs.shape, BF16),
        ),
        in_specs=[SMEM_SPEC] + [VMEM_SPEC] * 8,
        out_specs=[VMEM_SPEC] * 4,
        input_output_aliases={6: 1, 7: 2, 8: 3},
        compiler_params=pltpu.CompilerParams(vmem_limit_bytes=12 * 2**20),
        cost_estimate=pl.CostEstimate(flops=2**20, bytes_accessed=2**20, transcendentals=0),
        name="layer",
    )(
        where,
        in_vmem(x_in),
        in_vmem(start_x),
        in_vmem(gain),
        in_vmem(qkv),
        in_vmem(out),
        in_vmem(keys),
        in_vmem(values),
        in_vmem(outs),
    )


def shards(loaded, positions, span_lengths, visit_embed, w_query, w_key, w_value, w_out, norm_gain):
    width = loaded.shape[1]
    sections = lax.axis_size("section")
    chips = lax.axis_size("dp") // 2
    section = lax.axis_index("section")
    spot = lax.axis_index("dp")
    seq = loaded.shape[0] * sections
    att = w_query.shape[1]
    blocks = seq // ROWS

    right, left = lane_shift(chips, 1), lane_shift(chips, -1)
    sibling = [(i, i ^ 1) for i in range(2 * chips)]
    weights = [w_query, w_key, w_value, w_out]
    from_left = [lax.ppermute(w, "dp", right) for w in weights]
    from_right = [lax.ppermute(w, "dp", left) for w in weights]
    from_far = [
        lax.ppermute(from_left[k], "dp", right) if k % 2 == 0 else lax.ppermute(from_right[k], "dp", left)
        for k in range(4)
    ]
    pieces = []
    for k in range(4):
        group = []
        for piece in (weights[k], from_left[k], from_right[k], from_far[k]):
            group += [piece, lax.ppermute(piece, "dp", sibling)]
        pieces.append(group)

    tagged = jnp.concatenate(
        [loaded, jnp.broadcast_to(positions[:, None], (positions.shape[0], 128)).astype(BF16)], axis=1
    )
    gathered = lax.all_gather(tagged, "section", axis=0, tiled=True)
    owners = gathered[:, width].astype(jnp.int32)
    index = jnp.arange(seq, dtype=jnp.int32)
    placing = (index[:, None] == owners[None, :]).astype(BF16)
    ordered = jnp.dot(placing, gathered[:, :width], preferred_element_type=F32)
    lengths = span_lengths[0]
    ends = jnp.cumsum(lengths)
    visit = jnp.sum((index[:, None] >= ends[None, :]).astype(jnp.int32), axis=1)
    visit_hot = (visit[:, None] == jnp.arange(lengths.shape[0], dtype=jnp.int32)[None, :]).astype(BF16)
    start_x = (ordered + jnp.dot(visit_hot, visit_embed, preferred_element_type=F32)).astype(BF16)

    where = jnp.stack([spot // 2, spot % 2, section]).astype(jnp.int32)
    qkv, out = load_weights(spot // 2, spot % 2, pieces)
    keys = jnp.zeros((seq, att), BF16)
    values = jnp.zeros((seq, att), BF16)
    outs = jnp.zeros((seq, width), BF16)
    gain = norm_gain[None, :]
    arriving = {}
    zero = jnp.zeros((ROWS, width), BF16)
    for step in range(SKEW * (sections - 1) + blocks):
        x_in = arriving.pop(step, zero)
        y, keys, values, outs = run_step(
            step, blocks, where, x_in, start_x, gain, qkv, out, keys, values, outs
        )
        pairs = [
            (s, s + 1) for s in range(sections - 1) if 0 <= step - SKEW * s < blocks
        ]
        if pairs:
            arriving[step + SKEW] = lax.ppermute(y, "section", pairs)
    return outs[None]


def solution(mesh):
    placed = (
        P(("section", "dp"), None),
        P(("section", "dp")),
        P("dp", None),
        P(),
        P(("section", "dp"), None),
        P(("section", "dp"), None),
        P(("section", "dp"), None),
        P(("section", "dp"), None),
        P("section"),
    )
    return jax.shard_map(
        shards, mesh=mesh, in_specs=placed, out_specs=P("section", "dp", None), check_vma=False
    )
```

time: 1390 us -> 1070 us (0.77)
  waiting for transfers between devices: 924 us -> 85.2 us
  starting transfers between devices: 47.9 us -> 815 us
  local copies, waits for them, and re-layouts: 127 us -> 2.05 us
  Pallas kernels: 0 us -> 107 us
  loops' own time: 93.3 us -> 0 us
  matrix products: 75 us -> 0.7 us
  other arithmetic: 45.3 us -> 2.46 us
  blocking collectives: 65.5 us -> 47.7 us
    ppermute x37 -> x96, starting transfers between devices: 47.8 us -> 815 us  [the longest x68 775 us: shards(): arriving[step + SKEW] = lax.ppermute(y, 'section', pairs)]
    ppermute x37 -> x96, waiting for transfers between devices: 808 us -> 85.2 us  [the longest x4 33.8 us: shards(): from_right = [lax.ppermute(w, 'dp', left) for w in weights]]
    all_gather x4 -> x0, waiting for transfers between devices: 113 us -> none  [the longest x1 46.5 us: shards(): lax.all_gather(w_value, 'dp', axis=0, tiled=True)]
    pallas_call x0 -> x71, Pallas kernels: none -> 107 us  [the longest x70 97.5 us: run_step(): pl.pallas_call(body, out_shape=(pltpu.VMEM((ROWS, width), BF16), pltpu.VM...]
    another operation x38 -> x0, loops' own time: 93.3 us -> none  [the longest x1 79.1 us: shards(): final = lax.fori_loop(0, nchunk + depth_count - 1, turn, init)]
    dot_general x38 -> x2, matrix products: 75 us -> 0.7 us  [the longest x1 0.37 us: shards(): jnp.dot(visit_hot, visit_embed, preferred_element_type=F32)]
    dynamic_update_slice x49 -> x0, local copies, waits for them, and re-layouts: 60.7 us -> none  [the longest x37 51.9 us: turn(): out_buffer = lax.dynamic_update_slice_in_dim(out_buffer, keep, start, 0)]
    dynamic_slice x74 -> x0, local copies, waits for them, and re-layouts: 46.4 us -> none  [the longest x37 24.5 us: turn(): start = starts[safe]]
  transfers between devices with their start and end apart: 41 -> 96, of which waited for: 40 -> 19; matrix products, arithmetic and copies ran while one was open for 6% -> 0% of each run, Pallas kernels for 0% -> 9%
where the time goes in v1:
time: 1070 us; the launch traced here: 1060 us
  starting transfers between devices  815 us (76%)
  Pallas kernels  107 us (10%)
  waiting for transfers between devices  85.2 us (8%)
  blocking collectives  47.7 us (4%)
    ppermute x68, starting transfers between devices, shards(): arriving[step + SKEW] = lax.ppermute(y, 'section', pairs)  775 us
    pallas_call x70, Pallas kernels, run_step(): pl.pallas_call(body, out_shape=(pltpu.VMEM((ROWS, width), BF16), pltpu.VM...  97.5 us
    all_gather x1, blocking collectives, shards(): gathered = lax.all_gather(tagged, 'section', axis=0, tiled=True)  47.7 us
    ppermute x4, waiting for transfers between devices, shards(): from_right = [lax.ppermute(w, 'dp', left) for w in weights]  33.8 us
    ppermute x2, waiting for transfers between devices, shards(): lax.ppermute(from_right[k], 'dp', left)  30.7 us
  transfers between devices with their start and end apart: 96, of which 19 were waited for; matrix products, arithmetic and copies ran while one was open for 0% of the time, Pallas kernels for 9%

profile of v1, /device:TPU:248, one launch (start us, length us, event | category | flops | bytes accessed | tf_op | source)
XLA Modules:
  0.0 1061.1 jit_solution(3937929897500914117)
XLA Ops:
  80.7 17.2 %collective-permute-done.12.refs_14_ = bf16[320,1280]{1,0:T(8,128)(2,1)} collective-permute-done((bf16[320,1280]{1,0:T(8,128)(2,1)S(1)}, bf16[320,1280]{1,0:T(8,128)(2,1)}, u32[]{:S(2)}, u32[]{:S(2)}) %collective-permute-start.12) | collective-permute-done | bytes 819232 | tf_op jit(solution)/shard_map/ppermute | solution.py:173
  120.0 47.7 %all-gather = bf16[32,4,2688]{2,1,0:T(4,128)(2,1)S(1)} all-gather(bf16[1,4,2688]{2,1,0:T(4,128)(2,1)S(1)} %maximum_bitcast_fusion), channel_id=1, replica_groups=mesh['section'=32,'dp'=8] {'section'}, dimensions={0}, use_global_device_ids=true | all-gather | bytes 709632 | tf_op jit(solution)/shard_map/all_gather | solution.py:186
  225.3 77.2 %collective-permute-start.47 = (bf16[16,2560]{1,0:T(8,128)(2,1)S(1)}, bf16[16,2560]{1,0:T(8,128)(2,1)S(1)}, u32[]{:S(2)}, u32[]{:S(2)}) collective-permute-start(bf16[16,2560]{1,0:T(8,128)(2,1)S(1)} %get-tuple-element.361), channel_id=1, source_target_pairs={{48,56},{56,64},{64,72},{72,80},{49,57},{57,65},{65,73},{73,81},{5... | collective-permute-start | bytes 245768 | tf_op jit(solution)/shard_map/ppermute | solution.py:214
  304.5 19.7 %collective-permute-start.49 = (bf16[16,2560]{1,0:T(8,128)(2,1)S(1)}, bf16[16,2560]{1,0:T(8,128)(2,1)S(1)}, u32[]{:S(2)}, u32[]{:S(2)}) collective-permute-start(bf16[16,2560]{1,0:T(8,128)(2,1)S(1)} %get-tuple-element.369), channel_id=1, source_target_pairs={{56,64},{64,72},{72,80},{80,88},{57,65},{65,73},{73,81},{81,89},{5... | collective-permute-start | bytes 245768 | tf_op jit(solution)/shard_map/ppermute | solution.py:214
  554.1 16.9 %collective-permute-start.65 = (bf16[16,2560]{1,0:T(8,128)(2,1)S(1)}, bf16[16,2560]{1,0:T(8,128)(2,1)S(1)}, u32[]{:S(2)}, u32[]{:S(2)}) collective-permute-start(bf16[16,2560]{1,0:T(8,128)(2,1)S(1)} %get-tuple-element.433), channel_id=1, source_target_pairs={{120,128},{128,136},{136,144},{144,152},{121,129},{129,137},{137,1... | collective-permute-start | bytes 245768 | tf_op jit(solution)/shard_map/ppermute | solution.py:214
  571.7 17.5 %collective-permute-start.64 = (bf16[16,2560]{1,0:T(8,128)(2,1)S(1)}, bf16[16,2560]{1,0:T(8,128)(2,1)S(1)}, u32[]{:S(2)}, u32[]{:S(2)}) collective-permute-start(bf16[16,2560]{1,0:T(8,128)(2,1)S(1)} %get-tuple-element.432), channel_id=1, source_target_pairs={{120,128},{128,136},{136,144},{144,152},{121,129},{129,137},{137,1... | collective-permute-start | bytes 245768 | tf_op jit(solution)/shard_map/ppermute | solution.py:214
  589.8 17.5 %collective-permute-start.67 = (bf16[16,2560]{1,0:T(8,128)(2,1)S(1)}, bf16[16,2560]{1,0:T(8,128)(2,1)S(1)}, u32[]{:S(2)}, u32[]{:S(2)}) collective-permute-start(bf16[16,2560]{1,0:T(8,128)(2,1)S(1)} %get-tuple-element.441), channel_id=1, source_target_pairs={{128,136},{136,144},{144,152},{152,160},{129,137},{137,145},{145,1... | collective-permute-start | bytes 245768 | tf_op jit(solution)/shard_map/ppermute | solution.py:214
  607.9 17.5 %collective-permute-start.66 = (bf16[16,2560]{1,0:T(8,128)(2,1)S(1)}, bf16[16,2560]{1,0:T(8,128)(2,1)S(1)}, u32[]{:S(2)}, u32[]{:S(2)}) collective-permute-start(bf16[16,2560]{1,0:T(8,128)(2,1)S(1)} %get-tuple-element.440), channel_id=1, source_target_pairs={{128,136},{136,144},{144,152},{152,160},{129,137},{137,145},{145,1... | collective-permute-start | bytes 245768 | tf_op jit(solution)/shard_map/ppermute | solution.py:214
  626.4 17.5 %collective-permute-start.69 = (bf16[16,2560]{1,0:T(8,128)(2,1)S(1)}, bf16[16,2560]{1,0:T(8,128)(2,1)S(1)}, u32[]{:S(2)}, u32[]{:S(2)}) collective-permute-start(bf16[16,2560]{1,0:T(8,128)(2,1)S(1)} %get-tuple-element.449), channel_id=1, source_target_pairs={{136,144},{144,152},{152,160},{160,168},{137,145},{145,153},{153,1... | collective-permute-start | bytes 245768 | tf_op jit(solution)/shard_map/ppermute | solution.py:214
  644.5 17.5 %collective-permute-start.68 = (bf16[16,2560]{1,0:T(8,128)(2,1)S(1)}, bf16[16,2560]{1,0:T(8,128)(2,1)S(1)}, u32[]{:S(2)}, u32[]{:S(2)}) collective-permute-start(bf16[16,2560]{1,0:T(8,128)(2,1)S(1)} %get-tuple-element.448), channel_id=1, source_target_pairs={{136,144},{144,152},{152,160},{160,168},{137,145},{145,153},{153,1... | collective-permute-start | bytes 245768 | tf_op jit(solution)/shard_map/ppermute | solution.py:214
  662.6 17.5 %collective-permute-start.71 = (bf16[16,2560]{1,0:T(8,128)(2,1)S(1)}, bf16[16,2560]{1,0:T(8,128)(2,1)S(1)}, u32[]{:S(2)}, u32[]{:S(2)}) collective-permute-start(bf16[16,2560]{1,0:T(8,128)(2,1)S(1)} %get-tuple-element.457), channel_id=1, source_target_pairs={{144,152},{152,160},{160,168},{168,176},{145,153},{153,161},{161,1... | collective-permute-start | bytes 245768 | tf_op jit(solution)/shard_map/ppermute | solution.py:214
  680.9 17.5 %collective-permute-start.70 = (bf16[16,2560]{1,0:T(8,128)(2,1)S(1)}, bf16[16,2560]{1,0:T(8,128)(2,1)S(1)}, u32[]{:S(2)}, u32[]{:S(2)}) collective-permute-start(bf16[16,2560]{1,0:T(8,128)(2,1)S(1)} %get-tuple-element.456), channel_id=1, source_target_pairs={{144,152},{152,160},{160,168},{168,176},{145,153},{153,161},{161,1... | collective-permute-start | bytes 245768 | tf_op jit(solution)/shard_map/ppermute | solution.py:214
  699.0 17.3 %collective-permute-start.73 = (bf16[16,2560]{1,0:T(8,128)(2,1)S(1)}, bf16[16,2560]{1,0:T(8,128)(2,1)S(1)}, u32[]{:S(2)}, u32[]{:S(2)}) collective-permute-start(bf16[16,2560]{1,0:T(8,128)(2,1)S(1)} %get-tuple-element.465), channel_id=1, source_target_pairs={{152,160},{160,168},{168,176},{176,184},{153,161},{161,169},{169,1... | collective-permute-start | bytes 245768 | tf_op jit(solution)/shard_map/ppermute | solution.py:214
  716.8 17.3 %collective-permute-start.72 = (bf16[16,2560]{1,0:T(8,128)(2,1)S(1)}, bf16[16,2560]{1,0:T(8,128)(2,1)S(1)}, u32[]{:S(2)}, u32[]{:S(2)}) collective-permute-start(bf16[16,2560]{1,0:T(8,128)(2,1)S(1)} %get-tuple-element.464), channel_id=1, source_target_pairs={{152,160},{160,168},{168,176},{176,184},{153,161},{161,169},{169,1... | collective-permute-start | bytes 245768 | tf_op jit(solution)/shard_map/ppermute | solution.py:214
  734.9 16.9 %collective-permute-start.75 = (bf16[16,2560]{1,0:T(8,128)(2,1)S(1)}, bf16[16,2560]{1,0:T(8,128)(2,1)S(1)}, u32[]{:S(2)}, u32[]{:S(2)}) collective-permute-start(bf16[16,2560]{1,0:T(8,128)(2,1)S(1)} %get-tuple-element.473), channel_id=1, source_target_pairs={{160,168},{168,176},{176,184},{184,192},{161,169},{169,177},{177,1... | collective-permute-start | bytes 245768 | tf_op jit(solution)/shard_map/ppermute | solution.py:214
  752.4 16.9 %collective-permute-start.74 = (bf16[16,2560]{1,0:T(8,128)(2,1)S(1)}, bf16[16,2560]{1,0:T(8,128)(2,1)S(1)}, u32[]{:S(2)}, u32[]{:S(2)}) collective-permute-start(bf16[16,2560]{1,0:T(8,128)(2,1)S(1)} %get-tuple-element.472), channel_id=1, source_target_pairs={{160,168},{168,176},{176,184},{184,192},{161,169},{169,177},{177,1... | collective-permute-start | bytes 245768 | tf_op jit(solution)/shard_map/ppermute | solution.py:214
  769.9 16.9 %collective-permute-start.77 = (bf16[16,2560]{1,0:T(8,128)(2,1)S(1)}, bf16[16,2560]{1,0:T(8,128)(2,1)S(1)}, u32[]{:S(2)}, u32[]{:S(2)}) collective-permute-start(bf16[16,2560]{1,0:T(8,128)(2,1)S(1)} %get-tuple-element.481), channel_id=1, source_target_pairs={{168,176},{176,184},{184,192},{192,200},{169,177},{177,185},{185,1... | collective-permute-start | bytes 245768 | tf_op jit(solution)/shard_map/ppermute | solution.py:214
  787.7 16.9 %collective-permute-start.76 = (bf16[16,2560]{1,0:T(8,128)(2,1)S(1)}, bf16[16,2560]{1,0:T(8,128)(2,1)S(1)}, u32[]{:S(2)}, u32[]{:S(2)}) collective-permute-start(bf16[16,2560]{1,0:T(8,128)(2,1)S(1)} %get-tuple-element.480), channel_id=1, source_target_pairs={{168,176},{176,184},{184,192},{192,200},{169,177},{177,185},{185,1... | collective-permute-start | bytes 245768 | tf_op jit(solution)/shard_map/ppermute | solution.py:214
  805.2 16.9 %collective-permute-start.79 = (bf16[16,2560]{1,0:T(8,128)(2,1)S(1)}, bf16[16,2560]{1,0:T(8,128)(2,1)S(1)}, u32[]{:S(2)}, u32[]{:S(2)}) collective-permute-start(bf16[16,2560]{1,0:T(8,128)(2,1)S(1)} %get-tuple-element.489), channel_id=1, source_target_pairs={{176,184},{184,192},{192,200},{200,208},{177,185},{185,193},{193,2... | collective-permute-start | bytes 245768 | tf_op jit(solution)/shard_map/ppermute | solution.py:214
  822.7 16.9 %collective-permute-start.78 = (bf16[16,2560]{1,0:T(8,128)(2,1)S(1)}, bf16[16,2560]{1,0:T(8,128)(2,1)S(1)}, u32[]{:S(2)}, u32[]{:S(2)}) collective-permute-start(bf16[16,2560]{1,0:T(8,128)(2,1)S(1)} %get-tuple-element.488), channel_id=1, source_target_pairs={{176,184},{184,192},{192,200},{200,208},{177,185},{185,193},{193,2... | collective-permute-start | bytes 245768 | tf_op jit(solution)/shard_map/ppermute | solution.py:214
  840.3 16.7 %collective-permute-start.81 = (bf16[16,2560]{1,0:T(8,128)(2,1)S(1)}, bf16[16,2560]{1,0:T(8,128)(2,1)S(1)}, u32[]{:S(2)}, u32[]{:S(2)}) collective-permute-start(bf16[16,2560]{1,0:T(8,128)(2,1)S(1)} %get-tuple-element.497), channel_id=1, source_target_pairs={{184,192},{192,200},{200,208},{208,216},{185,193},{193,201},{201,2... | collective-permute-start | bytes 245768 | tf_op jit(solution)/shard_map/ppermute | solution.py:214
  857.5 16.7 %collective-permute-start.80 = (bf16[16,2560]{1,0:T(8,128)(2,1)S(1)}, bf16[16,2560]{1,0:T(8,128)(2,1)S(1)}, u32[]{:S(2)}, u32[]{:S(2)}) collective-permute-start(bf16[16,2560]{1,0:T(8,128)(2,1)S(1)} %get-tuple-element.496), channel_id=1, source_target_pairs={{184,192},{192,200},{200,208},{208,216},{185,193},{193,201},{201,2... | collective-permute-start | bytes 245768 | tf_op jit(solution)/shard_map/ppermute | solution.py:214
  874.8 16.3 %collective-permute-start.83 = (bf16[16,2560]{1,0:T(8,128)(2,1)S(1)}, bf16[16,2560]{1,0:T(8,128)(2,1)S(1)}, u32[]{:S(2)}, u32[]{:S(2)}) collective-permute-start(bf16[16,2560]{1,0:T(8,128)(2,1)S(1)} %get-tuple-element.505), channel_id=1, source_target_pairs={{192,200},{200,208},{208,216},{216,224},{193,201},{201,209},{209,2... | collective-permute-start | bytes 245768 | tf_op jit(solution)/shard_map/ppermute | solution.py:214
  908.7 16.3 %collective-permute-start.85 = (bf16[16,2560]{1,0:T(8,128)(2,1)S(1)}, bf16[16,2560]{1,0:T(8,128)(2,1)S(1)}, u32[]{:S(2)}, u32[]{:S(2)}) collective-permute-start(bf16[16,2560]{1,0:T(8,128)(2,1)S(1)} %get-tuple-element.513), channel_id=1, source_target_pairs={{200,208},{208,216},{216,224},{224,232},{201,209},{209,217},{217,2... | collective-permute-start | bytes 245768 | tf_op jit(solution)/shard_map/ppermute | solution.py:214
  (283 shorter events, 556.2 us)
Async XLA Ops:
  2.8 36.5 %collective-permute-start.24 = (bf16[160,2560]{1,0:T(8,128)(2,1)}, bf16[160,2560]{1,0:T(8,128)(2,1)}, u32[]{:S(2)}, u32[]{:S(2)}) collective-permute-start(bf16[160,2560]{1,0:T(8,128)(2,1)} %refs_24_.1), channel_id=1, source_target_pairs={{0,6},{1,7},{2,0},{3,1},{4,2},{5,3},{6,4},{7,5},{8,14},{9,15},{10,... | collective-permute-start | bytes 2457608 | tf_op jit(solution)/shard_map/ppermute | solution.py:171
  15.7 41.1 %collective-permute-start.17 = (bf16[320,1280]{1,0:T(8,128)(2,1)}, bf16[320,1280]{1,0:T(8,128)(2,1)}, u32[]{:S(2)}, u32[]{:S(2)}) collective-permute-start(bf16[320,1280]{1,0:T(8,128)(2,1)} %refs_16_.1), channel_id=1, source_target_pairs={{0,6},{1,7},{2,0},{3,1},{4,2},{5,3},{6,4},{7,5},{8,14},{9,15},{10,... | collective-permute-start | bytes 2457608 | tf_op jit(solution)/shard_map/ppermute | solution.py:171
  21.7 38.8 %collective-permute-start.22 = (bf16[160,2560]{1,0:T(8,128)(2,1)}, bf16[160,2560]{1,0:T(8,128)(2,1)}, u32[]{:S(2)}, u32[]{:S(2)}) collective-permute-start(bf16[160,2560]{1,0:T(8,128)(2,1)} %refs_24_.1), channel_id=1, source_target_pairs={{0,2},{1,3},{2,4},{3,5},{4,6},{5,7},{6,0},{7,1},{8,10},{9,11},{10,... | collective-permute-start | bytes 2457608 | tf_op jit(solution)/shard_map/ppermute | solution.py:170
  33.6 39.7 %collective-permute-start.3 = (bf16[320,1280]{1,0:T(8,128)(2,1)}, bf16[320,1280]{1,0:T(8,128)(2,1)}, u32[]{:S(2)}, u32[]{:S(2)}) collective-permute-start(bf16[320,1280]{1,0:T(8,128)(2,1)} %refs_0_.1), channel_id=1, source_target_pairs={{0,6},{1,7},{2,0},{3,1},{4,2},{5,3},{6,4},{7,5},{8,14},{9,15},{10,... | collective-permute-start | bytes 2457608 | tf_op jit(solution)/shard_map/ppermute | solution.py:171
  39.3 37.4 %collective-permute-start.8 = (bf16[320,1280]{1,0:T(8,128)(2,1)}, bf16[320,1280]{1,0:T(8,128)(2,1)}, u32[]{:S(2)}, u32[]{:S(2)}) collective-permute-start(bf16[320,1280]{1,0:T(8,128)(2,1)} %refs_8_.1), channel_id=1, source_target_pairs={{0,2},{1,3},{2,4},{3,5},{4,6},{5,7},{6,0},{7,1},{8,10},{9,11},{10,... | collective-permute-start | bytes 2457608 | tf_op jit(solution)/shard_map/ppermute | solution.py:170
  80.2 35.9 %collective-permute-start.5 = (bf16[320,1280]{1,0:T(8,128)(2,1)}, bf16[320,1280]{1,0:T(8,128)(2,1)S(1)}, u32[]{:S(2)}, u32[]{:S(2)}) collective-permute-start(bf16[320,1280]{1,0:T(8,128)(2,1)} %collective-permute-done.1.refs_2_), channel_id=1, source_target_pairs={{0,2},{1,3},{2,4},{3,5},{4,6},{5,7},{6,0},{7,1},{8,10},{9,11},{10,... | collective-permute-start | bytes 2457608 | tf_op jit(solution)/shard_map/ppermute | solution.py:173
  80.7 35.4 %collective-permute-start.11 = (bf16[320,1280]{1,0:T(8,128)(2,1)S(1)}, bf16[320,1280]{1,0:T(8,128)(2,1)S(1)}, u32[]{:S(2)}, u32[]{:S(2)}) collective-permute-start(bf16[320,1280]{1,0:T(8,128)(2,1)S(1)} %collective-permute-done.10.refs_12_), channel_id=1, source_target_pairs={{0,1},{1,0},{2,3},{3,2},{4,5},{5,4},{6,7},{7,6},{8,9},{9,8},{10,11... | collective-permute-start | bytes 2457608 | tf_op jit(solution)/shard_map/ppermute | solution.py:180
  99.3 68.3 %collective-permute-start.2 = (bf16[320,1280]{1,0:T(8,128)(2,1)}, bf16[320,1280]{1,0:T(8,128)(2,1)}, u32[]{:S(2)}, u32[]{:S(2)}) collective-permute-start(bf16[320,1280]{1,0:T(8,128)(2,1)} %collective-permute-done.1.refs_2_), channel_id=1, source_target_pairs={{0,1},{1,0},{2,3},{3,2},{4,5},{5,4},{6,7},{7,6},{8,9},{9,8},{10,11... | collective-permute-start | bytes 2457608 | tf_op jit(solution)/shard_map/ppermute | solution.py:180
  113.1 54.6 %collective-permute-start.25 = (bf16[160,2560]{1,0:T(8,128)(2,1)}, bf16[160,2560]{1,0:T(8,128)(2,1)}, u32[]{:S(2)}, u32[]{:S(2)}) collective-permute-start(bf16[160,2560]{1,0:T(8,128)(2,1)} %collective-permute-done.24.refs_28_), channel_id=1, source_target_pairs={{0,1},{1,0},{2,3},{3,2},{4,5},{5,4},{6,7},{7,6},{8,9},{9,8},{10,11... | collective-permute-start | bytes 2457608 | tf_op jit(solution)/shard_map/ppermute | solution.py:180
  116.1 52.1 %collective-permute-start.18 = (bf16[320,1280]{1,0:T(8,128)(2,1)}, bf16[320,1280]{1,0:T(8,128)(2,1)}, u32[]{:S(2)}, u32[]{:S(2)}) collective-permute-start(bf16[320,1280]{1,0:T(8,128)(2,1)} %collective-permute-done.17.refs_20_), channel_id=1, source_target_pairs={{0,1},{1,0},{2,3},{3,2},{4,5},{5,4},{6,7},{7,6},{8,9},{9,8},{10,11... | collective-permute-start | bytes 2457608 | tf_op jit(solution)/shard_map/ppermute | solution.py:180
  116.1 52.2 %collective-permute-start.23 = (bf16[160,2560]{1,0:T(8,128)(2,1)}, bf16[160,2560]{1,0:T(8,128)(2,1)}, u32[]{:S(2)}, u32[]{:S(2)}) collective-permute-start(bf16[160,2560]{1,0:T(8,128)(2,1)} %collective-permute-done.22.refs_26_), channel_id=1, source_target_pairs={{0,1},{1,0},{2,3},{3,2},{4,5},{5,4},{6,7},{7,6},{8,9},{9,8},{10,11... | collective-permute-start | bytes 2457608 | tf_op jit(solution)/shard_map/ppermute | solution.py:180
  116.6 52.1 %collective-permute-start.4 = (bf16[320,1280]{1,0:T(8,128)(2,1)}, bf16[320,1280]{1,0:T(8,128)(2,1)}, u32[]{:S(2)}, u32[]{:S(2)}) collective-permute-start(bf16[320,1280]{1,0:T(8,128)(2,1)} %collective-permute-done.3.refs_4_), channel_id=1, source_target_pairs={{0,1},{1,0},{2,3},{3,2},{4,5},{5,4},{6,7},{7,6},{8,9},{9,8},{10,11... | collective-permute-start | bytes 2457608 | tf_op jit(solution)/shard_map/ppermute | solution.py:180
  224.0 78.5 %collective-permute-start.44 = (bf16[16,2560]{1,0:T(8,128)(2,1)S(1)}, bf16[16,2560]{1,0:T(8,128)(2,1)S(1)}, u32[]{:S(2)}, u32[]{:S(2)}) collective-permute-start(bf16[16,2560]{1,0:T(8,128)(2,1)S(1)} %get-tuple-element.352), channel_id=1, source_target_pairs={{40,48},{48,56},{56,64},{64,72},{41,49},{49,57},{57,65},{65,73},{4... | collective-permute-start | bytes 245768 | tf_op jit(solution)/shard_map/ppermute | solution.py:214
  225.3 78.7 %collective-permute-start.47 = (bf16[16,2560]{1,0:T(8,128)(2,1)S(1)}, bf16[16,2560]{1,0:T(8,128)(2,1)S(1)}, u32[]{:S(2)}, u32[]{:S(2)}) collective-permute-start(bf16[16,2560]{1,0:T(8,128)(2,1)S(1)} %get-tuple-element.361), channel_id=1, source_target_pairs={{48,56},{56,64},{64,72},{72,80},{49,57},{57,65},{65,73},{73,81},{5... | collective-permute-start | bytes 245768 | tf_op jit(solution)/shard_map/ppermute | solution.py:214
  554.1 35.2 %collective-permute-start.65 = (bf16[16,2560]{1,0:T(8,128)(2,1)S(1)}, bf16[16,2560]{1,0:T(8,128)(2,1)S(1)}, u32[]{:S(2)}, u32[]{:S(2)}) collective-permute-start(bf16[16,2560]{1,0:T(8,128)(2,1)S(1)} %get-tuple-element.433), channel_id=1, source_target_pairs={{120,128},{128,136},{136,144},{144,152},{121,129},{129,137},{137,1... | collective-permute-start | bytes 245768 | tf_op jit(solution)/shard_map/ppermute | solution.py:214
  571.7 35.6 %collective-permute-start.64 = (bf16[16,2560]{1,0:T(8,128)(2,1)S(1)}, bf16[16,2560]{1,0:T(8,128)(2,1)S(1)}, u32[]{:S(2)}, u32[]{:S(2)}) collective-permute-start(bf16[16,2560]{1,0:T(8,128)(2,1)S(1)} %get-tuple-element.432), channel_id=1, source_target_pairs={{120,128},{128,136},{136,144},{144,152},{121,129},{129,137},{137,1... | collective-permute-start | bytes 245768 | tf_op jit(solution)/shard_map/ppermute | solution.py:214
  589.8 35.6 %collective-permute-start.67 = (bf16[16,2560]{1,0:T(8,128)(2,1)S(1)}, bf16[16,2560]{1,0:T(8,128)(2,1)S(1)}, u32[]{:S(2)}, u32[]{:S(2)}) collective-permute-start(bf16[16,2560]{1,0:T(8,128)(2,1)S(1)} %get-tuple-element.441), channel_id=1, source_target_pairs={{128,136},{136,144},{144,152},{152,160},{129,137},{137,145},{145,1... | collective-permute-start | bytes 245768 | tf_op jit(solution)/shard_map/ppermute | solution.py:214
  607.9 36.0 %collective-permute-start.66 = (bf16[16,2560]{1,0:T(8,128)(2,1)S(1)}, bf16[16,2560]{1,0:T(8,128)(2,1)S(1)}, u32[]{:S(2)}, u32[]{:S(2)}) collective-permute-start(bf16[16,2560]{1,0:T(8,128)(2,1)S(1)} %get-tuple-element.440), channel_id=1, source_target_pairs={{128,136},{136,144},{144,152},{152,160},{129,137},{137,145},{145,1... | collective-permute-start | bytes 245768 | tf_op jit(solution)/shard_map/ppermute | solution.py:214
  626.4 35.6 %collective-permute-start.69 = (bf16[16,2560]{1,0:T(8,128)(2,1)S(1)}, bf16[16,2560]{1,0:T(8,128)(2,1)S(1)}, u32[]{:S(2)}, u32[]{:S(2)}) collective-permute-start(bf16[16,2560]{1,0:T(8,128)(2,1)S(1)} %get-tuple-element.449), channel_id=1, source_target_pairs={{136,144},{144,152},{152,160},{160,168},{137,145},{145,153},{153,1... | collective-permute-start | bytes 245768 | tf_op jit(solution)/shard_map/ppermute | solution.py:214
  644.5 35.6 %collective-permute-start.68 = (bf16[16,2560]{1,0:T(8,128)(2,1)S(1)}, bf16[16,2560]{1,0:T(8,128)(2,1)S(1)}, u32[]{:S(2)}, u32[]{:S(2)}) collective-permute-start(bf16[16,2560]{1,0:T(8,128)(2,1)S(1)} %get-tuple-element.448), channel_id=1, source_target_pairs={{136,144},{144,152},{152,160},{160,168},{137,145},{145,153},{153,1... | collective-permute-start | bytes 245768 | tf_op jit(solution)/shard_map/ppermute | solution.py:214
  662.6 35.8 %collective-permute-start.71 = (bf16[16,2560]{1,0:T(8,128)(2,1)S(1)}, bf16[16,2560]{1,0:T(8,128)(2,1)S(1)}, u32[]{:S(2)}, u32[]{:S(2)}) collective-permute-start(bf16[16,2560]{1,0:T(8,128)(2,1)S(1)} %get-tuple-element.457), channel_id=1, source_target_pairs={{144,152},{152,160},{160,168},{168,176},{145,153},{153,161},{161,1... | collective-permute-start | bytes 245768 | tf_op jit(solution)/shard_map/ppermute | solution.py:214
  680.9 35.4 %collective-permute-start.70 = (bf16[16,2560]{1,0:T(8,128)(2,1)S(1)}, bf16[16,2560]{1,0:T(8,128)(2,1)S(1)}, u32[]{:S(2)}, u32[]{:S(2)}) collective-permute-start(bf16[16,2560]{1,0:T(8,128)(2,1)S(1)} %get-tuple-element.456), channel_id=1, source_target_pairs={{144,152},{152,160},{160,168},{168,176},{145,153},{153,161},{161,1... | collective-permute-start | bytes 245768 | tf_op jit(solution)/shard_map/ppermute | solution.py:214
  699.0 35.2 %collective-permute-start.73 = (bf16[16,2560]{1,0:T(8,128)(2,1)S(1)}, bf16[16,2560]{1,0:T(8,128)(2,1)S(1)}, u32[]{:S(2)}, u32[]{:S(2)}) collective-permute-start(bf16[16,2560]{1,0:T(8,128)(2,1)S(1)} %get-tuple-element.465), channel_id=1, source_target_pairs={{152,160},{160,168},{168,176},{176,184},{153,161},{161,169},{169,1... | collective-permute-start | bytes 245768 | tf_op jit(solution)/shard_map/ppermute | solution.py:214
  716.8 35.0 %collective-permute-start.72 = (bf16[16,2560]{1,0:T(8,128)(2,1)S(1)}, bf16[16,2560]{1,0:T(8,128)(2,1)S(1)}, u32[]{:S(2)}, u32[]{:S(2)}) collective-permute-start(bf16[16,2560]{1,0:T(8,128)(2,1)S(1)} %get-tuple-element.464), channel_id=1, source_target_pairs={{152,160},{160,168},{168,176},{176,184},{153,161},{161,169},{169,1... | collective-permute-start | bytes 245768 | tf_op jit(solution)/shard_map/ppermute | solution.py:214
  (84 other events, 2200.9 us)

commit v2 on v1

v2 whole, which is shorter than its diff:
```python
import jax
import jax.numpy as jnp
from jax import lax
from jax.experimental import pallas as pl
from jax.experimental.pallas import tpu as pltpu
from jax.sharding import PartitionSpec as P

HEADS = 16
GROUP = 8
ROWS = 16
SKEW = 2
WINDOW = 6
BF16 = jnp.bfloat16
F32 = jnp.float32


def in_vmem(value):
    return pltpu.with_memory_space_constraint(value, pltpu.VMEM)


def in_hbm(value):
    return pltpu.with_memory_space_constraint(value, pltpu.HBM)


VMEM_SPEC = pl.BlockSpec(memory_space=pltpu.VMEM)
HBM_SPEC = pl.BlockSpec(memory_space=pltpu.HBM)


def lane_shift(chips, steps):
    return [
        (x * 2 + c, ((x + steps) % chips) * 2 + c) for x in range(chips) for c in range(2)
    ]


def load_weights(pieces, shards_in_all):
    share = sum(p.shape[0] for _, away, other, p in pieces if away == 0 and other == 0)
    width = pieces[0][3].shape[1]

    def body(*refs):
        sources = refs[: len(pieces)]
        target, sems = refs[len(pieces) :]
        spot = lax.axis_index("dp")
        chip, core = spot // 2, lax.rem(spot, 2)
        copies = []
        for i, (first, away, other, piece) in enumerate(pieces):
            x = lax.rem(chip + away + 4, 4)
            c = core if other == 0 else 1 - core
            row = pl.multiple_of((x * 2 + c) * share + first, 16)
            copies.append(
                pltpu.make_async_copy(
                    sources[i], target.at[pl.ds(row, piece.shape[0]), :], sems.at[i]
                )
            )
        for copy in copies:
            copy.start()
        for copy in copies:
            copy.wait()

    flat = [in_hbm(piece[3]) for piece in pieces]
    return pl.pallas_call(
        body,
        out_shape=pltpu.VMEM((share * shards_in_all, width), BF16),
        in_specs=[HBM_SPEC] * len(flat),
        out_specs=VMEM_SPEC,
        scratch_shapes=[pltpu.SemaphoreType.DMA((len(flat),))],
        compiler_params=pltpu.CompilerParams(vmem_limit_bytes=2 * 2**20),
        name="load_weights",
    )(*flat)


def step_body(step, blocks, x_in, start_x, gain, masks, qkv, out, k_in, v_in, o_in, y, keys, values, outs):
    section = lax.axis_index("section")
    block = step - SKEW * section
    att, width = out.shape
    seq = keys.shape[0]
    size = att // HEADS
    wide = GROUP * size

    @pl.when((block >= 0) & (block < blocks))
    def _():
        row = pl.multiple_of(block * ROWS, ROWS)
        rows = pl.ds(row, ROWS)
        first = (jnp.zeros((ROWS, width), jnp.int32) + section) == 0
        x = jnp.where(first, start_x[rows, :].astype(F32), x_in[...].astype(F32))
        normed = (
            x * lax.rsqrt(jnp.mean(x * x, axis=1, keepdims=True) + 1e-05) * gain[...]
        ).astype(BF16)
        mixed = jnp.dot(normed, qkv[...], preferred_element_type=F32).astype(BF16)
        query = mixed[:, :att]
        keys[rows, :] = mixed[:, att : 2 * att]
        values[rows, :] = mixed[:, 2 * att :]
        mask = masks[...]
        key_at = lax.broadcasted_iota(jnp.int32, (GROUP, ROWS, seq), 2)
        query_at = lax.broadcasted_iota(jnp.int32, (GROUP, ROWS, seq), 1) + row
        allowed = (key_at <= query_at).reshape(GROUP * ROWS, seq)
        joined = []
        for g in range(HEADS // GROUP):
            cols = slice(g * wide, (g + 1) * wide)
            spread = (query[:, cols][None] * mask.astype(BF16)[:, None, :]).reshape(GROUP * ROWS, wide)
            scores = lax.dot_general(
                spread, keys[:, cols], (((1,), (1,)), ((), ())), preferred_element_type=F32
            )
            scores = jnp.where(allowed, scores * (size**-0.5), -1e30)
            powers = jnp.exp(scores - jnp.max(scores, axis=1, keepdims=True))
            probs = (powers * (1.0 / jnp.sum(powers, axis=1, keepdims=True))).astype(BF16)
            mixed_v = jnp.dot(probs, values[:, cols], preferred_element_type=F32)
            mixed_v = mixed_v.reshape(GROUP, ROWS, wide) * mask[:, None, :]
            joined.append(jnp.sum(mixed_v, axis=0).astype(BF16))
        attended = jnp.concatenate(joined, axis=1)
        result = (x + jnp.dot(attended, out[...], preferred_element_type=F32)).astype(BF16)
        y[...] = result
        outs[rows, :] = result


def run_step(step, blocks, x_in, start_x, gain, masks, qkv, out, keys, values, outs):
    width = out.shape[1]

    def body(*refs):
        step_body(step, blocks, *refs)

    operands = (x_in, start_x, gain, masks, qkv, out, keys, values, outs)
    return pl.pallas_call(
        body,
        out_shape=(
            pltpu.VMEM((ROWS, width), BF16),
            pltpu.VMEM(keys.shape, BF16),
            pltpu.VMEM(values.shape, BF16),
            pltpu.VMEM(outs.shape, BF16),
        ),
        in_specs=[VMEM_SPEC] * len(operands),
        out_specs=[VMEM_SPEC] * 4,
        input_output_aliases={6: 1, 7: 2, 8: 3},
        compiler_params=pltpu.CompilerParams(vmem_limit_bytes=12 * 2**20),
        cost_estimate=pl.CostEstimate(flops=2**20, bytes_accessed=2**20, transcendentals=0),
        name="layer",
    )(*[in_vmem(operand) for operand in operands])


def after(value, *events):
    return lax.optimization_barrier((value, *events))[0]


def shards(loaded, positions, span_lengths, visit_embed, w_query, w_key, w_value, w_out, norm_gain):
    width = loaded.shape[1]
    sections = lax.axis_size("section")
    chips = lax.axis_size("dp") // 2
    seq = loaded.shape[0] * sections
    att = w_query.shape[1]
    blocks = seq // ROWS

    right, left = lane_shift(chips, 1), lane_shift(chips, -1)
    sibling = [(i, i ^ 1) for i in range(2 * chips)]
    shares = (jnp.concatenate([w_query, w_key, w_value], axis=1), w_out)
    from_left = [lax.ppermute(share, "dp", right) for share in shares]
    from_right = [lax.ppermute(share, "dp", left) for share in shares]
    others = [None, lax.ppermute(w_out, "dp", sibling)]

    tagged = jnp.concatenate(
        [loaded, jnp.broadcast_to(positions[:, None], (positions.shape[0], 128)).astype(BF16)], axis=1
    )
    gathered = lax.all_gather(after(tagged, others[1]), "section", axis=0, tiled=True)
    owners = gathered[:, width].astype(jnp.int32)
    index = jnp.arange(seq, dtype=jnp.int32)
    placing = (index[:, None] == owners[None, :]).astype(BF16)
    ordered = jnp.dot(placing, gathered[:, :width], preferred_element_type=F32)
    lengths = span_lengths[0]
    ends = jnp.cumsum(lengths)
    visit = jnp.sum((index[:, None] >= ends[None, :]).astype(jnp.int32), axis=1)
    visit_hot = (visit[:, None] == jnp.arange(lengths.shape[0], dtype=jnp.int32)[None, :]).astype(BF16)
    start_x = (ordered + jnp.dot(visit_hot, visit_embed, preferred_element_type=F32)).astype(BF16)

    loaded_weights = []
    for k, share in enumerate(shares):
        half = share.shape[0] // 2
        far = [
            (0, 2, lax.ppermute(after(from_left[k][:half], start_x), "dp", right)),
            (half, 2, lax.ppermute(after(from_right[k][half:], start_x), "dp", left)),
        ]
        pieces = []
        for first, away, got in ((0, 0, share), (0, -1, from_left[k]), (0, 1, from_right[k]), *far):
            other = others[k] if away == 0 else None
            if other is None:
                other = lax.ppermute(after(got, start_x), "dp", sibling)
            pieces.append((first, away, 0, got))
            pieces.append((first, away, 1, other))
        loaded_weights.append(load_weights(pieces, 2 * chips))

    wide = GROUP * (att // HEADS)
    masks = (
        jnp.arange(wide, dtype=jnp.int32)[None, :] // (att // HEADS)
        == jnp.arange(GROUP, dtype=jnp.int32)[:, None]
    ).astype(F32)
    qkv, out = loaded_weights
    keys = jnp.zeros((seq, att), BF16)
    values = jnp.zeros((seq, att), BF16)
    outs = jnp.zeros((seq, width), BF16)
    gain = norm_gain[None, :]
    arriving = {}
    nothing = jnp.zeros((ROWS, width), BF16)
    last = SKEW * (sections - 1) + blocks
    for step in range(last):
        x_in = arriving.pop(step, nothing)
        y, keys, values, outs = run_step(
            step, blocks, x_in, start_x, gain, masks, qkv, out, keys, values, outs
        )
        if step + SKEW < last:
            base = step // WINDOW * WINDOW
            pairs = [
                (s, s + 1)
                for s in range(sections - 1)
                if any(0 <= t - SKEW * s < blocks for t in range(base, base + WINDOW))
            ]
            arriving[step + SKEW] = lax.ppermute(y, "section", pairs)
    return outs[None]


def solution(mesh):
    placed = (
        P(("section", "dp"), None),
        P(("section", "dp")),
        P("dp", None),
        P(),
        P(("section", "dp"), None),
        P(("section", "dp"), None),
        P(("section", "dp"), None),
        P(("section", "dp"), None),
        P("section"),
    )
    return jax.shard_map(
        shards, mesh=mesh, in_specs=placed, out_specs=P("section", "dp", None), check_vma=False
    )
```

time: 1070 us -> 512 us (0.48)
  starting transfers between devices: 815 us -> 63.9 us
  waiting for transfers between devices: 85.2 us -> 221 us
  Pallas kernels: 107 us -> 146 us
  local copies, waits for them, and re-layouts: 2.05 us -> 17.6 us
    ppermute x68, starting transfers between devices: 775 us -> 50.3 us  [shards(): arriving[step + SKEW] = lax.ppermute(y, 'section', pairs)]
    ppermute x68, waiting for transfers between devices: 1.57 us -> 173 us  [shards(): arriving[step + SKEW] = lax.ppermute(y, 'section', pairs)]
    pallas_call x70, Pallas kernels: 97.5 us -> 137 us  [run_step(): pl.pallas_call(body, out_shape=(pltpu.VMEM((ROWS, width), BF16), pltpu.VM...]
    ppermute x28 -> x18, waiting for transfers between devices: 83.6 us -> 48 us  [the longest x2 30.6 us: shards(): lax.ppermute(after(from_left[k][:half], start_x), 'dp', right)]
    ppermute x28 -> x18, starting transfers between devices: 39.3 us -> 13.7 us  [the longest x2 4.7 us: shards(): from_right = [lax.ppermute(share, 'dp', left) for share in shares]]
  transfers between devices with their start and end apart: 96 -> 86, of which waited for: 19 -> 13; matrix products, arithmetic and copies ran while one was open for 0% -> 2% of each run, Pallas kernels for 9% -> 27%
where the time goes in v2:
time: 512 us; the launch traced here: 502 us
  waiting for transfers between devices  221 us (43%)
  Pallas kernels  146 us (29%)
  starting transfers between devices  63.9 us (12%)
  blocking collectives  47.4 us (9%)
  local copies, waits for them, and re-layouts  17.6 us (3%)
    ppermute x68, waiting for transfers between devices, shards(): arriving[step + SKEW] = lax.ppermute(y, 'section', pairs)  173 us
    pallas_call x70, Pallas kernels, run_step(): pl.pallas_call(body, out_shape=(pltpu.VMEM((ROWS, width), BF16), pltpu.VM...  137 us
    ppermute x68, starting transfers between devices, shards(): arriving[step + SKEW] = lax.ppermute(y, 'section', pairs)  50.3 us
    all_gather x1, blocking collectives, shards(): lax.all_gather(after(tagged, others[1]), 'section', axis=0, tiled=True)  47.4 us
    ppermute x2, waiting for transfers between devices, shards(): lax.ppermute(after(from_left[k][:half], start_x), 'dp', right)  30.6 us
    ppermute x2, waiting for transfers between devices, shards(): from_left = [lax.ppermute(share, 'dp', right) for share in shares]  13.8 us
    unnamed x49, local copies, waits for them, and re-layouts  12.1 us
  transfers between devices with their start and end apart: 86, of which 13 were waited for; matrix products, arithmetic and copies ran while one was open for 2% of the time, Pallas kernels for 27%

profile of v2, /device:TPU:248, one launch (start us, length us, event | category | flops | bytes accessed | tf_op | source)
XLA Modules:
  0.0 502.1 jit_solution(2724961200240738527)
XLA Ops:
  14.7 47.4 %all-gather = bf16[32,4,2688]{2,1,0:T(4,128)(2,1)S(1)} all-gather(bf16[1,4,2688]{2,1,0:T(4,128)(2,1)S(1)} %bitcast.9), channel_id=1, replica_groups=mesh['section'=32,'dp'=8] {'section'}, dimensions={0}, use_global_device_ids=true | all-gather | bytes 709632 | tf_op jit(solution)/shard_map/all_gather | solution.py:161
  65.8 13.8 %collective-permute-done.10.refs_2_ = bf16[160,2560]{1,0:T(8,128)(2,1)} collective-permute-done((bf16[160,2560]{1,0:T(8,128)(2,1)}, bf16[160,2560]{1,0:T(8,128)(2,1)}, u32[]{:S(2)}, u32[]{:S(2)}) %collective-permute-start.10) | collective-permute-done | bytes 819232 | tf_op jit(solution)/shard_map/ppermute | solution.py:154
  86.9 7.3 %collective-permute-done.14.refs_6_ = bf16[80,2560]{1,0:T(8,128)(2,1)S(1)} collective-permute-done((bf16[80,2560]{1,0:T(8,128)(2,1)S(1)}, bf16[80,2560]{1,0:T(8,128)(2,1)S(1)}, u32[]{:S(2)}, u32[]{:S(2)}) %collective-permute-start.14) | collective-permute-done | bytes 409632 | tf_op jit(solution)/shard_map/ppermute | solution.py:176
  96.8 23.3 %collective-permute-done.6.refs_6_ = bf16[160,3840]{1,0:T(8,128)(2,1)S(1)} collective-permute-done((bf16[160,3840]{1,0:T(8,128)(2,1)S(1)}, bf16[160,3840]{1,0:T(8,128)(2,1)S(1)}, u32[]{:S(2)}, u32[]{:S(2)}) %collective-permute-start.6) | collective-permute-done | bytes 1228832 | tf_op jit(solution)/shard_map/ppermute | solution.py:176
  132.6 6.7 %load_weights.2.refs_4_ = bf16[2560,3840]{1,0:T(8,128)(2,1)S(1)} custom-call(bf16[320,3840]{1,0:T(8,128)(2,1)} %constant_dynamic-update-slice_fusion.refs_0_, bf16[320,3840]{1,0:T(8,128)(2,1)} %copy-done.3, bf16[320,3840]{1,0:T(8,128)(2,1)} %copy-done.2, bf16[320,3840]{1,0:T(8,128)(2,1)} %copy-done.4, bf16[320,3840]{1,0:T(8,128)(2,1)} %collective-permute-done.4.refs_4_, ...), custom_call_target="tpu_custom_call" | custom-call | tf_op jit(solution)/shard_map/load_weights/pallas_call | solution.py:60
  144.1 5.1 %layer.76 = (bf16[16,2560]{1,0:T(8,128)(2,1)S(1)}, bf16[128,1280]{1,0:T(8,128)(2,1)S(1)}, bf16[128,1280]{1,0:T(8,128)(2,1)S(1)}, bf16[128,2560]{1,0:T(8,128)(2,1)S(1)}) custom-call(bf16[16,2560]{1,0:T(8,128)(2,1)S(1)} %collective-permute-done.23.refs_0_, ...), custom_call_target="tpu_custom_call", output_to_operand_aliasing={{1}: (6, {}), {2}: (7, {}), {3}: (8, {})} | custom-call | flops 1048576 | bytes 1048576 | tf_op jit(solution)/shard_map/layer/pallas_call | solution.py:122
  151.3 5.1 %layer.79 = (bf16[16,2560]{1,0:T(8,128)(2,1)S(1)}, bf16[128,1280]{1,0:T(8,128)(2,1)S(1)}, bf16[128,1280]{1,0:T(8,128)(2,1)S(1)}, bf16[128,2560]{1,0:T(8,128)(2,1)S(1)}) custom-call(bf16[16,2560]{1,0:T(8,128)(2,1)S(1)} %collective-permute-done.24.refs_0_, ...), custom_call_target="tpu_custom_call", output_to_operand_aliasing={{1}: (6, {}), {2}: (7, {}), {3}: (8, {})} | custom-call | flops 1048576 | bytes 1048576 | tf_op jit(solution)/shard_map/layer/pallas_call | solution.py:122
  158.5 5.3 %layer.82 = (bf16[16,2560]{1,0:T(8,128)(2,1)S(1)}, bf16[128,1280]{1,0:T(8,128)(2,1)S(1)}, bf16[128,1280]{1,0:T(8,128)(2,1)S(1)}, bf16[128,2560]{1,0:T(8,128)(2,1)S(1)}) custom-call(bf16[16,2560]{1,0:T(8,128)(2,1)S(1)} %collective-permute-done.29.refs_0_, ...), custom_call_target="tpu_custom_call", output_to_operand_aliasing={{1}: (6, {}), {2}: (7, {}), {3}: (8, {})} | custom-call | flops 1048576 | bytes 1048576 | tf_op jit(solution)/shard_map/layer/pallas_call | solution.py:122
  165.9 5.1 %layer.85 = (bf16[16,2560]{1,0:T(8,128)(2,1)S(1)}, bf16[128,1280]{1,0:T(8,128)(2,1)S(1)}, bf16[128,1280]{1,0:T(8,128)(2,1)S(1)}, bf16[128,2560]{1,0:T(8,128)(2,1)S(1)}) custom-call(bf16[16,2560]{1,0:T(8,128)(2,1)S(1)} %collective-permute-done.30.refs_0_, ...), custom_call_target="tpu_custom_call", output_to_operand_aliasing={{1}: (6, {}), {2}: (7, {}), {3}: (8, {})} | custom-call | flops 1048576 | bytes 1048576 | tf_op jit(solution)/shard_map/layer/pallas_call | solution.py:122
  173.1 5.1 %layer.88 = (bf16[16,2560]{1,0:T(8,128)(2,1)S(1)}, bf16[128,1280]{1,0:T(8,128)(2,1)S(1)}, bf16[128,1280]{1,0:T(8,128)(2,1)S(1)}, bf16[128,2560]{1,0:T(8,128)(2,1)S(1)}) custom-call(bf16[16,2560]{1,0:T(8,128)(2,1)S(1)} %collective-permute-done.35.refs_0_, ...), custom_call_target="tpu_custom_call", output_to_operand_aliasing={{1}: (6, {}), {2}: (7, {}), {3}: (8, {})} | custom-call | flops 1048576 | bytes 1048576 | tf_op jit(solution)/shard_map/layer/pallas_call | solution.py:122
  180.3 5.3 %layer.91 = (bf16[16,2560]{1,0:T(8,128)(2,1)S(1)}, bf16[128,1280]{1,0:T(8,128)(2,1)S(1)}, bf16[128,1280]{1,0:T(8,128)(2,1)S(1)}, bf16[128,2560]{1,0:T(8,128)(2,1)S(1)}) custom-call(bf16[16,2560]{1,0:T(8,128)(2,1)S(1)} %collective-permute-done.36.refs_0_, ...), custom_call_target="tpu_custom_call", output_to_operand_aliasing={{1}: (6, {}), {2}: (7, {}), {3}: (8, {})} | custom-call | flops 1048576 | bytes 1048576 | tf_op jit(solution)/shard_map/layer/pallas_call | solution.py:122
  187.8 5.1 %layer.94 = (bf16[16,2560]{1,0:T(8,128)(2,1)S(1)}, bf16[128,1280]{1,0:T(8,128)(2,1)S(1)}, bf16[128,1280]{1,0:T(8,128)(2,1)S(1)}, bf16[128,2560]{1,0:T(8,128)(2,1)S(1)}) custom-call(bf16[16,2560]{1,0:T(8,128)(2,1)S(1)} %collective-permute-done.41.refs_0_, ...), custom_call_target="tpu_custom_call", output_to_operand_aliasing={{1}: (6, {}), {2}: (7, {}), {3}: (8, {})} | custom-call | flops 1048576 | bytes 1048576 | tf_op jit(solution)/shard_map/layer/pallas_call | solution.py:122
  195.0 5.1 %layer.97 = (bf16[16,2560]{1,0:T(8,128)(2,1)S(1)}, bf16[128,1280]{1,0:T(8,128)(2,1)S(1)}, bf16[128,1280]{1,0:T(8,128)(2,1)S(1)}, bf16[128,2560]{1,0:T(8,128)(2,1)S(1)}) custom-call(bf16[16,2560]{1,0:T(8,128)(2,1)S(1)} %collective-permute-done.42.refs_0_, ...), custom_call_target="tpu_custom_call", output_to_operand_aliasing={{1}: (6, {}), {2}: (7, {}), {3}: (8, {})} | custom-call | flops 1048576 | bytes 1048576 | tf_op jit(solution)/shard_map/layer/pallas_call | solution.py:122
  202.2 5.3 %layer.100 = (bf16[16,2560]{1,0:T(8,128)(2,1)S(1)}, bf16[128,1280]{1,0:T(8,128)(2,1)S(1)}, bf16[128,1280]{1,0:T(8,128)(2,1)S(1)}, bf16[128,2560]{1,0:T(8,128)(2,1)S(1)}) custom-call(bf16[16,2560]{1,0:T(8,128)(2,1)S(1)} %collective-permute-done.47.refs_0_, ...), custom_call_target="tpu_custom_call", output_to_operand_aliasing={{1}: (6, {}), {2}: (7, {}), {3}: (8, {})} | custom-call | flops 1048576 | bytes 1048576 | tf_op jit(solution)/shard_map/layer/pallas_call | solution.py:122
  209.6 5.1 %layer.103 = (bf16[16,2560]{1,0:T(8,128)(2,1)S(1)}, bf16[128,1280]{1,0:T(8,128)(2,1)S(1)}, bf16[128,1280]{1,0:T(8,128)(2,1)S(1)}, bf16[128,2560]{1,0:T(8,128)(2,1)S(1)}) custom-call(bf16[16,2560]{1,0:T(8,128)(2,1)S(1)} %collective-permute-done.48.refs_0_, ...), custom_call_target="tpu_custom_call", output_to_operand_aliasing={{1}: (6, {}), {2}: (7, {}), {3}: (8, {})} | custom-call | flops 1048576 | bytes 1048576 | tf_op jit(solution)/shard_map/layer/pallas_call | solution.py:122
  216.8 5.1 %layer.106 = (bf16[16,2560]{1,0:T(8,128)(2,1)S(1)}, bf16[128,1280]{1,0:T(8,128)(2,1)S(1)}, bf16[128,1280]{1,0:T(8,128)(2,1)S(1)}, bf16[128,2560]{1,0:T(8,128)(2,1)S(1)}) custom-call(bf16[16,2560]{1,0:T(8,128)(2,1)S(1)} %collective-permute-done.53.refs_0_, ...), custom_call_target="tpu_custom_call", output_to_operand_aliasing={{1}: (6, {}), {2}: (7, {}), {3}: (8, {})} | custom-call | flops 1048576 | bytes 1048576 | tf_op jit(solution)/shard_map/layer/pallas_call | solution.py:122
  224.0 5.3 %layer.109 = (bf16[16,2560]{1,0:T(8,128)(2,1)S(1)}, bf16[128,1280]{1,0:T(8,128)(2,1)S(1)}, bf16[128,1280]{1,0:T(8,128)(2,1)S(1)}, bf16[128,2560]{1,0:T(8,128)(2,1)S(1)}) custom-call(bf16[16,2560]{1,0:T(8,128)(2,1)S(1)} %collective-permute-done.54.refs_0_, ...), custom_call_target="tpu_custom_call", output_to_operand_aliasing={{1}: (6, {}), {2}: (7, {}), {3}: (8, {})} | custom-call | flops 1048576 | bytes 1048576 | tf_op jit(solution)/shard_map/layer/pallas_call | solution.py:122
  231.4 5.1 %layer.112 = (bf16[16,2560]{1,0:T(8,128)(2,1)S(1)}, bf16[128,1280]{1,0:T(8,128)(2,1)S(1)}, bf16[128,1280]{1,0:T(8,128)(2,1)S(1)}, bf16[128,2560]{1,0:T(8,128)(2,1)S(1)}) custom-call(bf16[16,2560]{1,0:T(8,128)(2,1)S(1)} %collective-permute-done.59.refs_0_, ...), custom_call_target="tpu_custom_call", output_to_operand_aliasing={{1}: (6, {}), {2}: (7, {}), {3}: (8, {})} | custom-call | flops 1048576 | bytes 1048576 | tf_op jit(solution)/shard_map/layer/pallas_call | solution.py:122
  238.6 5.1 %layer.115 = (bf16[16,2560]{1,0:T(8,128)(2,1)S(1)}, bf16[128,1280]{1,0:T(8,128)(2,1)S(1)}, bf16[128,1280]{1,0:T(8,128)(2,1)S(1)}, bf16[128,2560]{1,0:T(8,128)(2,1)S(1)}) custom-call(bf16[16,2560]{1,0:T(8,128)(2,1)S(1)} %collective-permute-done.60.refs_0_, ...), custom_call_target="tpu_custom_call", output_to_operand_aliasing={{1}: (6, {}), {2}: (7, {}), {3}: (8, {})} | custom-call | flops 1048576 | bytes 1048576 | tf_op jit(solution)/shard_map/layer/pallas_call | solution.py:122
  245.9 5.3 %layer.118 = (bf16[16,2560]{1,0:T(8,128)(2,1)S(1)}, bf16[128,1280]{1,0:T(8,128)(2,1)S(1)}, bf16[128,1280]{1,0:T(8,128)(2,1)S(1)}, bf16[128,2560]{1,0:T(8,128)(2,1)S(1)}) custom-call(bf16[16,2560]{1,0:T(8,128)(2,1)S(1)} %collective-permute-done.65.refs_0_, ...), custom_call_target="tpu_custom_call", output_to_operand_aliasing={{1}: (6, {}), {2}: (7, {}), {3}: (8, {})} | custom-call | flops 1048576 | bytes 1048576 | tf_op jit(solution)/shard_map/layer/pallas_call | solution.py:122
  260.5 5.1 %layer.124 = (bf16[16,2560]{1,0:T(8,128)(2,1)S(1)}, bf16[128,1280]{1,0:T(8,128)(2,1)S(1)}, bf16[128,1280]{1,0:T(8,128)(2,1)S(1)}, bf16[128,2560]{1,0:T(8,128)(2,1)S(1)}) custom-call(bf16[16,2560]{1,0:T(8,128)(2,1)S(1)} %collective-permute-done.71.refs_0_, ...), custom_call_target="tpu_custom_call", output_to_operand_aliasing={{1}: (6, {}), {2}: (7, {}), {3}: (8, {})} | custom-call | flops 1048576 | bytes 1048576 | tf_op jit(solution)/shard_map/layer/pallas_call | solution.py:122
  267.7 5.3 %layer.127 = (bf16[16,2560]{1,0:T(8,128)(2,1)S(1)}, bf16[128,1280]{1,0:T(8,128)(2,1)S(1)}, bf16[128,1280]{1,0:T(8,128)(2,1)S(1)}, bf16[128,2560]{1,0:T(8,128)(2,1)S(1)}) custom-call(bf16[16,2560]{1,0:T(8,128)(2,1)S(1)} %collective-permute-done.72.refs_0_, ...), custom_call_target="tpu_custom_call", output_to_operand_aliasing={{1}: (6, {}), {2}: (7, {}), {3}: (8, {})} | custom-call | flops 1048576 | bytes 1048576 | tf_op jit(solution)/shard_map/layer/pallas_call | solution.py:122
  282.9 165.9 %collective-permute-done.79.refs_0_ = bf16[16,2560]{1,0:T(8,128)(2,1)S(1)} collective-permute-done((bf16[16,2560]{1,0:T(8,128)(2,1)S(1)}, bf16[16,2560]{1,0:T(8,128)(2,1)S(1)}, u32[]{:S(2)}, u32[]{:S(2)}) %collective-permute-start.79) | collective-permute-done | bytes 81952 | tf_op jit(solution)/shard_map/ppermute | solution.py:213
  495.5 5.3 %layer.139 = (bf16[16,2560]{1,0:T(8,128)(2,1)}, bf16[128,1280]{1,0:T(8,128)(2,1)S(1)}, bf16[128,1280]{1,0:T(8,128)(2,1)S(1)}, bf16[128,2560]{1,0:T(8,128)(2,1)S(1)}) custom-call(bf16[16,2560]{1,0:T(8,128)(2,1)S(1)} %collective-permute-done.84.refs_0_, bf16[128,2560]{1,0:T(8,128)(2,1)S(1)} %fusion.refs_1_, ...), custom_call_target="tpu_custom_call", output_to_operand_aliasing={{1}: (6, {}), {2}: (7, {}), {3}: (8, {})} | custom-call | flops 1048576 | bytes 1048576 | tf_op jit(solution)/shard_map/layer/pallas_call | solution.py:122
  (291 shorter events, 142.2 us)
Async XLA Ops:
  5.4 77.8 %collective-permute-start.2 = (bf16[320,3840]{1,0:T(8,128)(2,1)}, bf16[320,3840]{1,0:T(8,128)(2,1)S(1)}, u32[]{:S(2)}, u32[]{:S(2)}) collective-permute-start(bf16[320,3840]{1,0:T(8,128)(2,1)} %constant_dynamic-update-slice_fusion.refs_0_), channel_id=1, source_target_pairs={{0,2},{1,3},{2,4},{3,5},{4,6},{5,7},{6,0},{7,1},{8,10},{9,11},{10,... | collective-permute-start | bytes 7372808 | tf_op jit(solution)/shard_map/ppermute | solution.py:154
  6.9 78.5 %collective-permute-start.4 = (bf16[320,3840]{1,0:T(8,128)(2,1)}, bf16[320,3840]{1,0:T(8,128)(2,1)}, u32[]{:S(2)}, u32[]{:S(2)}) collective-permute-start(bf16[320,3840]{1,0:T(8,128)(2,1)} %constant_dynamic-update-slice_fusion.refs_0_), channel_id=1, source_target_pairs={{0,6},{1,7},{2,0},{3,1},{4,2},{5,3},{6,4},{7,5},{8,14},{9,15},{10,... | collective-permute-start | bytes 7372808 | tf_op jit(solution)/shard_map/ppermute | solution.py:155
  8.6 70.9 %collective-permute-start.10 = (bf16[160,2560]{1,0:T(8,128)(2,1)}, bf16[160,2560]{1,0:T(8,128)(2,1)}, u32[]{:S(2)}, u32[]{:S(2)}) collective-permute-start(bf16[160,2560]{1,0:T(8,128)(2,1)} %refs_0_.1), channel_id=1, source_target_pairs={{0,2},{1,3},{2,4},{3,5},{4,6},{5,7},{6,0},{7,1},{8,10},{9,11},{10,... | collective-permute-start | bytes 2457608 | tf_op jit(solution)/shard_map/ppermute | solution.py:154
  8.9 70.7 %collective-permute-start.12 = (bf16[160,2560]{1,0:T(8,128)(2,1)}, bf16[160,2560]{1,0:T(8,128)(2,1)}, u32[]{:S(2)}, u32[]{:S(2)}) collective-permute-start(bf16[160,2560]{1,0:T(8,128)(2,1)} %refs_0_.1), channel_id=1, source_target_pairs={{0,6},{1,7},{2,0},{3,1},{4,2},{5,3},{6,4},{7,5},{8,14},{9,15},{10,... | collective-permute-start | bytes 2457608 | tf_op jit(solution)/shard_map/ppermute | solution.py:155
  79.6 16.5 %collective-permute-start.11 = (bf16[160,2560]{1,0:T(8,128)(2,1)}, bf16[160,2560]{1,0:T(8,128)(2,1)S(1)}, u32[]{:S(2)}, u32[]{:S(2)}) collective-permute-start(bf16[160,2560]{1,0:T(8,128)(2,1)} %collective-permute-done.10.refs_2_), channel_id=1, source_target_pairs={{0,1},{1,0},{2,3},{3,2},{4,5},{5,4},{6,7},{7,6},{8,9},{9,8},{10,11... | collective-permute-start | bytes 2457608 | tf_op jit(solution)/shard_map/ppermute | solution.py:183
  80.6 13.5 %collective-permute-start.14 = (bf16[80,2560]{1,0:T(8,128)(2,1)S(1)}, bf16[80,2560]{1,0:T(8,128)(2,1)S(1)}, u32[]{:S(2)}, u32[]{:S(2)}) collective-permute-start(bf16[80,2560]{1,0:T(8,128)(2,1)S(1)} %slice.28), channel_id=1, source_target_pairs={{0,2},{1,3},{2,4},{3,5},{4,6},{5,7},{6,0},{7,1},{8,10},{9,11},{10,... | collective-permute-start | bytes 1228808 | tf_op jit(solution)/shard_map/ppermute | solution.py:176
  82.2 14.5 %collective-permute-start.13 = (bf16[160,2560]{1,0:T(8,128)(2,1)}, bf16[160,2560]{1,0:T(8,128)(2,1)S(1)}, u32[]{:S(2)}, u32[]{:S(2)}) collective-permute-start(bf16[160,2560]{1,0:T(8,128)(2,1)} %collective-permute-done.12.refs_4_), channel_id=1, source_target_pairs={{0,1},{1,0},{2,3},{3,2},{4,5},{5,4},{6,7},{7,6},{8,9},{9,8},{10,11... | collective-permute-start | bytes 2457608 | tf_op jit(solution)/shard_map/ppermute | solution.py:183
  83.2 12.8 %collective-permute-start.16 = (bf16[80,2560]{1,0:T(8,128)(2,1)S(1)}, bf16[80,2560]{1,0:T(8,128)(2,1)S(1)}, u32[]{:S(2)}, u32[]{:S(2)}) collective-permute-start(bf16[80,2560]{1,0:T(8,128)(2,1)S(1)} %slice.29), channel_id=1, source_target_pairs={{0,6},{1,7},{2,0},{3,1},{4,2},{5,3},{6,4},{7,5},{8,14},{9,15},{10,... | collective-permute-start | bytes 1228808 | tf_op jit(solution)/shard_map/ppermute | solution.py:177
  85.4 34.7 %collective-permute-start.6 = (bf16[160,3840]{1,0:T(8,128)(2,1)S(1)}, bf16[160,3840]{1,0:T(8,128)(2,1)S(1)}, u32[]{:S(2)}, u32[]{:S(2)}) collective-permute-start(bf16[160,3840]{1,0:T(8,128)(2,1)S(1)} %slice.26), channel_id=1, source_target_pairs={{0,2},{1,3},{2,4},{3,5},{4,6},{5,7},{6,0},{7,1},{8,10},{9,11},{10,... | collective-permute-start | bytes 3686408 | tf_op jit(solution)/shard_map/ppermute | solution.py:176
  94.2 28.3 %collective-permute-start.8 = (bf16[160,3840]{1,0:T(8,128)(2,1)S(1)}, bf16[160,3840]{1,0:T(8,128)(2,1)S(1)}, u32[]{:S(2)}, u32[]{:S(2)}) collective-permute-start(bf16[160,3840]{1,0:T(8,128)(2,1)S(1)} %slice.27), channel_id=1, source_target_pairs={{0,6},{1,7},{2,0},{3,1},{4,2},{5,3},{6,4},{7,5},{8,14},{9,15},{10,... | collective-permute-start | bytes 3686408 | tf_op jit(solution)/shard_map/ppermute | solution.py:177
  96.0 32.1 %collective-permute-start.1 = (bf16[320,3840]{1,0:T(8,128)(2,1)}, bf16[320,3840]{1,0:T(8,128)(2,1)S(1)}, u32[]{:S(2)}, u32[]{:S(2)}) collective-permute-start(bf16[320,3840]{1,0:T(8,128)(2,1)} %constant_dynamic-update-slice_fusion.refs_0_), channel_id=1, source_target_pairs={{0,1},{1,0},{2,3},{3,2},{4,5},{5,4},{6,7},{7,6},{8,9},{9,8},{10,11... | collective-permute-start | bytes 7372808 | tf_op jit(solution)/shard_map/ppermute | solution.py:183
  96.1 32.1 %collective-permute-start.3 = (bf16[320,3840]{1,0:T(8,128)(2,1)S(1)}, bf16[320,3840]{1,0:T(8,128)(2,1)S(1)}, u32[]{:S(2)}, u32[]{:S(2)}) collective-permute-start(bf16[320,3840]{1,0:T(8,128)(2,1)S(1)} %collective-permute-done.2.refs_2_), channel_id=1, source_target_pairs={{0,1},{1,0},{2,3},{3,2},{4,5},{5,4},{6,7},{7,6},{8,9},{9,8},{10,11... | collective-permute-start | bytes 7372808 | tf_op jit(solution)/shard_map/ppermute | solution.py:183
  96.6 31.6 %collective-permute-start.5 = (bf16[320,3840]{1,0:T(8,128)(2,1)}, bf16[320,3840]{1,0:T(8,128)(2,1)S(1)}, u32[]{:S(2)}, u32[]{:S(2)}) collective-permute-start(bf16[320,3840]{1,0:T(8,128)(2,1)} %collective-permute-done.4.refs_4_), channel_id=1, source_target_pairs={{0,1},{1,0},{2,3},{3,2},{4,5},{5,4},{6,7},{7,6},{8,9},{9,8},{10,11... | collective-permute-start | bytes 7372808 | tf_op jit(solution)/shard_map/ppermute | solution.py:183
  157.8 6.7 %collective-permute-start.28 = (bf16[16,2560]{1,0:T(8,128)(2,1)S(1)}, bf16[16,2560]{1,0:T(8,128)(2,1)S(1)}, u32[]{:S(2)}, u32[]{:S(2)}) collective-permute-start(bf16[16,2560]{1,0:T(8,128)(2,1)S(1)} %get-tuple-element.352), channel_id=1, source_target_pairs={{0,8},{8,16},{16,24},{24,32},{32,40},{40,48},{1,9},{9,17},{17,25},... | collective-permute-start | bytes 245768 | tf_op jit(solution)/shard_map/ppermute | solution.py:213
  179.7 6.7 %collective-permute-start.39 = (bf16[16,2560]{1,0:T(8,128)(2,1)S(1)}, bf16[16,2560]{1,0:T(8,128)(2,1)S(1)}, u32[]{:S(2)}, u32[]{:S(2)}) collective-permute-start(bf16[16,2560]{1,0:T(8,128)(2,1)S(1)} %get-tuple-element.393), channel_id=1, source_target_pairs={{48,56},{56,64},{64,72},{72,80},{80,88},{88,96},{49,57},{57,65},{6... | collective-permute-start | bytes 245768 | tf_op jit(solution)/shard_map/ppermute | solution.py:213
  274.4 7.1 %collective-permute-start.76 = (bf16[16,2560]{1,0:T(8,128)(2,1)S(1)}, bf16[16,2560]{1,0:T(8,128)(2,1)S(1)}, u32[]{:S(2)}, u32[]{:S(2)}) collective-permute-start(bf16[16,2560]{1,0:T(8,128)(2,1)S(1)} %get-tuple-element.544), channel_id=1, source_target_pairs={{192,200},{200,208},{208,216},{216,224},{224,232},{232,240},{193,2... | collective-permute-start | bytes 245768 | tf_op jit(solution)/shard_map/ppermute | solution.py:213
  280.2 168.5 %collective-permute-start.79 = (bf16[16,2560]{1,0:T(8,128)(2,1)S(1)}, bf16[16,2560]{1,0:T(8,128)(2,1)S(1)}, u32[]{:S(2)}, u32[]{:S(2)}) collective-permute-start(bf16[16,2560]{1,0:T(8,128)(2,1)S(1)} %get-tuple-element.553), channel_id=1, source_target_pairs={{216,224},{224,232},{232,240},{240,248},{217,225},{225,233},{233,2... | collective-permute-start | bytes 245768 | tf_op jit(solution)/shard_map/ppermute | solution.py:213
  281.6 174.1 %collective-permute-start.78 = (bf16[16,2560]{1,0:T(8,128)(2,1)S(1)}, bf16[16,2560]{1,0:T(8,128)(2,1)S(1)}, u32[]{:S(2)}, u32[]{:S(2)}) collective-permute-start(bf16[16,2560]{1,0:T(8,128)(2,1)S(1)} %get-tuple-element.552), channel_id=1, source_target_pairs={{216,224},{224,232},{232,240},{240,248},{217,225},{225,233},{233,2... | collective-permute-start | bytes 245768 | tf_op jit(solution)/shard_map/ppermute | solution.py:213
  453.2 9.0 %collective-permute-start.81 = (bf16[16,2560]{1,0:T(8,128)(2,1)S(1)}, bf16[16,2560]{1,0:T(8,128)(2,1)S(1)}, u32[]{:S(2)}, u32[]{:S(2)}) collective-permute-start(bf16[16,2560]{1,0:T(8,128)(2,1)S(1)} %get-tuple-element.561), channel_id=1, source_target_pairs={{216,224},{224,232},{232,240},{240,248},{217,225},{225,233},{233,2... | collective-permute-start | bytes 245768 | tf_op jit(solution)/shard_map/ppermute | solution.py:213
  460.2 8.7 %collective-permute-start.80 = (bf16[16,2560]{1,0:T(8,128)(2,1)S(1)}, bf16[16,2560]{1,0:T(8,128)(2,1)S(1)}, u32[]{:S(2)}, u32[]{:S(2)}) collective-permute-start(bf16[16,2560]{1,0:T(8,128)(2,1)S(1)} %get-tuple-element.560), channel_id=1, source_target_pairs={{216,224},{224,232},{232,240},{240,248},{217,225},{225,233},{233,2... | collective-permute-start | bytes 245768 | tf_op jit(solution)/shard_map/ppermute | solution.py:213
  466.6 9.8 %collective-permute-start.83 = (bf16[16,2560]{1,0:T(8,128)(2,1)S(1)}, bf16[16,2560]{1,0:T(8,128)(2,1)S(1)}, u32[]{:S(2)}, u32[]{:S(2)}) collective-permute-start(bf16[16,2560]{1,0:T(8,128)(2,1)S(1)} %get-tuple-element.569), channel_id=1, source_target_pairs={{216,224},{224,232},{232,240},{240,248},{217,225},{225,233},{233,2... | collective-permute-start | bytes 245768 | tf_op jit(solution)/shard_map/ppermute | solution.py:213
  473.4 10.0 %collective-permute-start.82 = (bf16[16,2560]{1,0:T(8,128)(2,1)S(1)}, bf16[16,2560]{1,0:T(8,128)(2,1)S(1)}, u32[]{:S(2)}, u32[]{:S(2)}) collective-permute-start(bf16[16,2560]{1,0:T(8,128)(2,1)S(1)} %get-tuple-element.568), channel_id=1, source_target_pairs={{216,224},{224,232},{232,240},{240,248},{217,225},{225,233},{233,2... | collective-permute-start | bytes 245768 | tf_op jit(solution)/shard_map/ppermute | solution.py:213
  481.0 8.4 %collective-permute-start.85 = (bf16[16,2560]{1,0:T(8,128)(2,1)S(1)}, bf16[16,2560]{1,0:T(8,128)(2,1)S(1)}, u32[]{:S(2)}, u32[]{:S(2)}) collective-permute-start(bf16[16,2560]{1,0:T(8,128)(2,1)S(1)} %get-tuple-element.577), channel_id=1, source_target_pairs={{240,248},{241,249},{242,250},{243,251},{244,252},{245,253},{246,2... | collective-permute-start | bytes 245768 | tf_op jit(solution)/shard_map/ppermute | solution.py:213
  487.8 7.7 %collective-permute-start.84 = (bf16[16,2560]{1,0:T(8,128)(2,1)S(1)}, bf16[16,2560]{1,0:T(8,128)(2,1)S(1)}, u32[]{:S(2)}, u32[]{:S(2)}) collective-permute-start(bf16[16,2560]{1,0:T(8,128)(2,1)S(1)} %get-tuple-element.576), channel_id=1, source_target_pairs={{240,248},{241,249},{242,250},{243,251},{244,252},{245,253},{246,2... | collective-permute-start | bytes 245768 | tf_op jit(solution)/shard_map/ppermute | solution.py:213
  (84 other events, 437.6 us)
